TPU v7x, 32 devices: a whole 2x2x4 slice. The times are simulated.
32 devices in a mesh: row: 4 (over y, x), col: 8 (over z, core).
Axes of the slice: x: 2, y: 2, z: 4, core: 2. Of those that a mesh axis runs over, the one named last changes fastest.
Arguments:
- chol: bfloat16 [6000, 8192], P('row', 'col'), may hold values from -1.75 to 1.75
- amplitudes: bfloat16 [8192, 4096], P('col', 'row'), may hold values from -0.0625 to 0.0625
- pair_offsets: int32 [4], replicated, may hold values from 0 to 8064
Outputs:
- residual: float32 [512, 4096], P('col', 'row')
All inputs are finite; a program needn't handle non-finite values.
Results may differ from a plain program's by a relative error of at most 0.003.
Values may be sent and summed in bfloat16 or wider, within the bound.
No kernel may reach another device: no remote copies, remote signals or barrier semaphores. Data moves between devices by JAX's collectives and lax.ppermute only.
A program may use at most 64 MiB of HBM per device.

v0:
```python
import functools

import jax
import jax.numpy as jnp
from jax import lax
from jax.experimental import pallas as pl
from jax.experimental.pallas import tpu as pltpu
from jax.sharding import PartitionSpec as P

AB_TILE = 128
SPLIT = (5, 3)
PAD = 16
AXES = ("row", "col")
VMEM = pltpu.CompilerParams(vmem_limit_bytes=20 * 1024 * 1024)


def pairs(rows, cols, target):
    listed = []
    for row in range(rows):
        for col in range(cols):
            to = target(row, col // 2, col % 2)
            listed.append((row * cols + col, to[0] * cols + to[1] * 2 + to[2]))
    return listed


def entry(offsets, chip, width, index):
    low = chip * (2 * width)
    seen = jnp.int32(0)
    block = jnp.int32(0)
    for b in range(offsets.shape[0]):
        start = offsets[b]
        here = ((start < low + 2 * width) & (start + (AB_TILE - 1) >= low)).astype(jnp.int32)
        block = jnp.where((here == 1) & (seen == index), b, block)
        seen = seen + here
    return block, seen > index


def pick_kernel(base, part, share, offsets, chol, keep, give, *most):
    cap, unit, depth = keep.shape
    width = chol.shape[1]
    col = lax.axis_index("col")
    chip, core = lax.div(col, 2), lax.rem(col, 2)
    window = 2 * AB_TILE
    t = lax.broadcasted_iota(jnp.int32, (unit, window), 0)
    lane = lax.broadcasted_iota(jnp.int32, (unit, window), 1)
    place = lax.div(t, part) * share + base + lax.rem(t, part)
    for slot in range(cap):
        for ref, parity in ((give, 1 - core), (keep, core)):
            block, there = entry(offsets, chip, width, 2 * slot + parity)
            start = offsets[block] - col * width
            left = jnp.clip(lax.shift_right_arithmetic(start, 7), 0, width // AB_TILE - 2)
            left = pl.multiple_of(left * AB_TILE, AB_TILE)
            start = jnp.where(there, start, -4 * AB_TILE - width)
            hit = (lane + left == place + start).astype(jnp.float32).astype(jnp.bfloat16)
            ref[slot] = lax.dot_general(
                hit,
                chol[:, pl.ds(left, window)],
                (((1,), (1,)), ((), ())),
                preferred_element_type=jnp.float32,
            ).astype(jnp.bfloat16)
    for ref in most:
        value = jnp.int32(0)
        for place in range(lax.axis_size("col") // 2):
            low = place * 2 * width
            seen = jnp.int32(0)
            for b in range(offsets.shape[0]):
                here = (offsets[b] < low + 2 * width) & (offsets[b] + (AB_TILE - 1) >= low)
                seen = seen + here.astype(jnp.int32)
            value = jnp.maximum(value, seen)
        ref[0] = value


def integrals_kernel(places, offsets, *refs):
    mine, other = refs[:places], refs[places : 2 * places]
    chol, block_out, factors = refs[2 * places :]
    cap, unit, depth = mine[0].shape
    width = chol.shape[1]
    col = lax.axis_index("col")
    chip, core = lax.div(col, 2), lax.rem(col, 2)
    factors[...] = jnp.zeros_like(factors)
    for j in range(places):
        for group, parity in ((mine, core), (other, 1 - core)):
            for slot in range(cap):
                block, there = entry(offsets, lax.bitwise_xor(chip, j), width, 2 * slot + parity)

                @pl.when(there)
                def _():
                    at = pl.ds(pl.multiple_of(block * unit, unit), unit)
                    factors[at, :] += group[j][slot]

    height = factors.shape[0]
    value = jnp.dot(factors[...], chol[...], preferred_element_type=jnp.float32)
    top = jnp.max(jnp.max(jnp.abs(value), axis=0, keepdims=True), axis=1, keepdims=True)
    power = jnp.floor(14.0 - jnp.log2(jnp.maximum(top, 1e-30)))
    power = jnp.broadcast_to(jnp.clip(power, -100.0, 100.0), (1, width))
    block_out[:height, :] = value * jnp.exp2(power)
    block_out[height:, :] = jnp.broadcast_to(power, (PAD, width))


def join_kernel(own, came, total):
    height = own.shape[0] - PAD
    first, second = own[height : height + 1, :], came[height : height + 1, :]
    power = jnp.minimum(first, second) - 1.0
    total[:height, :] = own[:height, :] * jnp.exp2(power - first) + came[:height, :] * jnp.exp2(power - second)
    total[height:, :] = jnp.broadcast_to(power, (PAD, own.shape[1]))


def residual_kernel(own, came, amplitudes, keep, give, result):
    core = lax.rem(lax.axis_index("col"), 2)
    places, part, _ = keep.shape
    height = own.shape[0] - PAD
    first, second = own[height : height + 1, :], came[height : height + 1, :]
    block = own[:height, :] * jnp.exp2(-first) + came[:height, :] * jnp.exp2(-second)
    result[...] = jnp.dot(
        block.astype(jnp.bfloat16), amplitudes[...], preferred_element_type=jnp.float32
    )
    for p in range(places):
        keep[p] = result[pl.ds(pl.multiple_of(p * 2 * part + core * part, part), part), :]
        give[p] = result[pl.ds(pl.multiple_of(p * 2 * part + (1 - core) * part, part), part), :]


def split_kernel(keep, came, own, *gives):
    chip = lax.div(lax.axis_index("col"), 2)
    own[...] = keep[chip] + came[chip]
    for j, give in enumerate(gives, 1):
        to = lax.bitwise_xor(chip, j)
        give[...] = (keep[to] + came[to]).astype(jnp.bfloat16)


def final_kernel(terms, *refs):
    out = refs[-1]
    base = 0
    for h in range(len(SPLIT)):
        group = refs[h * terms : (h + 1) * terms]
        value = group[0][...]
        for ref in group[1:]:
            value = value + ref[...].astype(jnp.float32)
        out[base : base + value.shape[0], :] = value
        base += value.shape[0]


def call(kernel, outs, smem, *args, scratch=(), flops=0):
    size = sum(a.size * a.dtype.itemsize for a in args)
    place = lambda o: pl.BlockSpec(memory_space=pltpu.SMEM if o.dtype == jnp.int32 else pltpu.VMEM)
    return pl.pallas_call(
        kernel,
        out_shape=outs,
        out_specs=jax.tree.map(place, outs),
        in_specs=[pl.BlockSpec(memory_space=pltpu.SMEM)] * smem
        + [pl.BlockSpec(memory_space=pltpu.VMEM)] * (len(args) - smem),
        scratch_shapes=list(scratch),
        compiler_params=VMEM,
        cost_estimate=pl.CostEstimate(flops=flops, bytes_accessed=size, transcendentals=0),
    )(*args)


def make(rows, cols):
    places = cols // 2
    bits = 2
    swap_core = pairs(rows, cols, lambda r, z, k: (r, z, 1 - k))
    in_plane = [
        pairs(rows, cols, lambda r, z, k, j=j: (r ^ (1 << (j if k == 0 else bits - 1 - j)), z, k))
        for j in range(bits)
    ]
    jumps = [pairs(rows, cols, lambda r, z, k, j=j: (r, z ^ j, k)) for j in range(places)]

    def on_device(chol, amplitudes, pair_offsets):
        depth, width = chol.shape
        columns = amplitudes.shape[1]
        blocks = pair_offsets.shape[0]
        share = blocks * AB_TILE // cols
        parts = [share * eighths // 8 for eighths in SPLIT]

        def picked(cap, h, offsets, most=()):
            held = jax.ShapeDtypeStruct((cap, AB_TILE // share * parts[h], depth), jnp.bfloat16)
            kernel = functools.partial(pick_kernel, sum(parts[:h]), parts[h], share)
            keep, give, *most = call(kernel, (held, held, *most), 1, offsets, chol)
            return (keep + lax.ppermute(give, AXES, swap_core), *most)

        def rest(cap, own):
            def jump(own, j):
                return lax.ppermute(own, AXES, jumps[j])

            def integrals(mine):
                height = blocks * mine[0].shape[1]
                other = [lax.ppermute(m, AXES, swap_core) for m in mine]
                return call(
                    functools.partial(integrals_kernel, places),
                    jax.ShapeDtypeStruct((height + PAD, width), jnp.float32),
                    1,
                    pair_offsets,
                    *mine,
                    *other,
                    chol,
                    scratch=[pltpu.VMEM((height, depth), jnp.bfloat16)],
                    flops=2 * height * depth * width,
                )

            def swap(block, j):
                came = lax.ppermute(block.astype(jnp.float16), AXES, in_plane[j])
                return came.astype(jnp.float32)

            def join(block, came):
                return call(join_kernel, jax.ShapeDtypeStruct(block.shape, jnp.float32), 0, block, came)

            def residual(block, came, part):
                height = block.shape[0] - PAD
                return call(
                    residual_kernel,
                    (jax.ShapeDtypeStruct((places, part, columns), jnp.float32),) * 2,
                    0,
                    block,
                    came,
                    amplitudes,
                    scratch=[pltpu.VMEM((height, columns), jnp.float32)],
                    flops=2 * height * width * columns,
                )

            def split(keep, got):
                part = keep.shape[1]
                return call(
                    split_kernel,
                    (jax.ShapeDtypeStruct((part, columns), jnp.float32),)
                    + (jax.ShapeDtypeStruct((part, columns), jnp.bfloat16),) * (places - 1),
                    0,
                    keep,
                    got,
                )

            def deliver(gives):
                return [lax.ppermute(g, AXES, jumps[j]) for j, g in enumerate(gives, 1)]

            after = lax.optimization_barrier
            mine = [own] + [jump(own, j) for j in range(1, places)]
            offsets, _ = after((pair_offsets, mine[1]))
            (own,) = picked(cap, 1, offsets)
            own, *mine = after((own, *mine))
            block = integrals(mine)
            far = jump(own, places - 1)
            came = swap(block, 0)
            came, far = after((came, far))
            block = join(block, came)
            near, _ = after((own, block))
            near = [jump(near, j) for j in range(1, places - 1)]
            came = swap(block, 1)
            keep, give = residual(block, came, parts[0])
            got = lax.ppermute(give, AXES, swap_core)
            own, far, *near, _ = after((own, far, *near, give))
            second = integrals([own, *near, far])
            second, _ = after((second, came))
            came = swap(second, 0)
            sums, *gives = split(keep, got)
            done = [sums] + deliver(gives)
            second = join(second, came)
            second, *done = after((second, *done))
            came = swap(second, 1)
            keep, give = residual(second, came, parts[1])
            sums, *gives = split(keep, lax.ppermute(give, AXES, swap_core))
            done += [sums] + deliver(gives)
            return call(
                functools.partial(final_kernel, places),
                jax.ShapeDtypeStruct((share, columns), jnp.float32),
                0,
                *done,
            )

        own, most = picked(1, 0, pair_offsets, (jax.ShapeDtypeStruct((1,), jnp.int32),))
        return lax.cond(
            most[0] <= 2,
            lambda own: rest(1, own),
            lambda own: rest((blocks + 1) // 2, *picked((blocks + 1) // 2, 0, pair_offsets)),
            own,
        )

    return on_device


def simple(chol, amplitudes, pair_offsets):
    width = chol.shape[1]
    rows = (pair_offsets[:, None] + jnp.arange(AB_TILE, dtype=jnp.int32)[None, :]).reshape(-1)
    local = lax.axis_index("col") * width + jnp.arange(width, dtype=jnp.int32)
    selector = (local[:, None] == rows[None, :]).astype(jnp.bfloat16)
    picked = jnp.dot(chol, selector, preferred_element_type=jnp.float32)
    factors = lax.psum(picked.astype(jnp.bfloat16), "col")
    block = jnp.dot(factors.T, chol, preferred_element_type=jnp.float32)
    block = lax.psum(block, "row").astype(jnp.bfloat16)
    return lax.psum_scatter(
        jnp.dot(block, amplitudes, preferred_element_type=jnp.float32),
        "col",
        scatter_dimension=0,
        tiled=True,
    )


def solution(mesh):
    rows, cols = mesh.shape["row"], mesh.shape["col"]
    body = make(rows, cols) if (rows, cols) == (4, 8) else simple
    return jax.shard_map(
        body,
        mesh=mesh,
        in_specs=(P("row", "col"), P("col", "row"), P()),
        out_specs=P("col", "row"),
        check_vma=False,
    )
```

profile of v0, /device:TPU:0, one launch (start us, length us, event | category | flops | bytes accessed | tf_op | source)
XLA Modules:
  0.0 97.8 jit_solution(10435963785589450393)
XLA Ops:
  0.0 3.0 %shard_map.39 = (bf16[1,80,1500]{2,1,0:T(8,128)(2,1)S(1)}, bf16[1,80,1500]{2,1,0:T(8,128)(2,1)S(1)}, s32[1]{0:T(128)}) custom-call(s32[4]{0:T(128)} %offsets.1, bf16[1500,1024]{1,0:T(8,128)(2,1)} %chol.1), custom_call_target="tpu_custom_call" | custom-call | bytes 3072016 | tf_op jit(solution)/shard_map/pallas_call | solution.py:145
  3.0 0.5 collective-permute-start.55
  4.2 0.5 collective-permute-done.55
  4.7 92.4 %conditional.1 = (f32[64,1024]{1,0:T(8,128)S(1)}) conditional(s32[]{:T(128)} %bitcast, (s32[4]{0:T(128)S(1)}, bf16[1500,1024]{1,0:T(8,128)(2,1)S(1)}, bf16[1024,1024]{1,0:T(8,128)(2,1)}) %tuple.34, (bf16[1,80,1500]{2,1,0:T(8,128)(2,1)S(1)}, bf16[1,80,1500]{2,1,0:T(8,128)(2,1)S(1)}, s32[4]{0:T(128)S(1)}, bf16[1500,1024]{1,0:T(8,128)(2,1)S(1)}, ...), branch_computations={%region_0.0_spmd, %region_1.0_spmd} | conditional | flops 2649218048 | bytes 97610952 | solution.py:268
  4.7 0.1 add.11.refs_0_
  4.8 3.0 %collective-permute-start.28 = (bf16[1,80,1500]{2,1,0:T(8,128)(2,1)S(1)}, bf16[1,80,1500]{2,1,0:T(8,128)(2,1)S(1)}, u32[]{:S(2)}, u32[]{:S(2)}) collective-permute-start(bf16[1,80,1500]{2,1,0:T(8,128)(2,1)S(1)} %add.11.refs_0_), channel_id=1, source_target_pairs={{0,2},{1,3},{2,0},{3,1},{4,6},{5,7},{6,4},{7,5},{8,10},{9,11},{10,... | collective-permute-start | bytes 720008 | tf_op jit(solution)/shard_map/cond/branch_1_fun/ppermute | solution.py:182
  7.8 2.6 %collective-permute-start.30 = (bf16[1,80,1500]{2,1,0:T(8,128)(2,1)S(1)}, bf16[1,80,1500]{2,1,0:T(8,128)(2,1)S(1)}, u32[]{:S(2)}, u32[]{:S(2)}) collective-permute-start(bf16[1,80,1500]{2,1,0:T(8,128)(2,1)S(1)} %add.11.refs_0_), channel_id=1, source_target_pairs={{0,4},{1,5},{2,6},{3,7},{4,0},{5,1},{6,2},{7,3},{8,12},{9,13},{10,... | collective-permute-start | bytes 720008 | tf_op jit(solution)/shard_map/cond/branch_1_fun/ppermute | solution.py:182
  10.4 8.3 %collective-permute-done.28.refs_1_ = bf16[1,80,1500]{2,1,0:T(8,128)(2,1)S(1)} collective-permute-done((bf16[1,80,1500]{2,1,0:T(8,128)(2,1)S(1)}, bf16[1,80,1500]{2,1,0:T(8,128)(2,1)S(1)}, u32[]{:S(2)}, u32[]{:S(2)}) %collective-permute-start.28) | collective-permute-done | bytes 240032 | tf_op jit(solution)/shard_map/cond/branch_1_fun/ppermute | solution.py:182
  18.7 1.1 %branch_1_fun.10 = (bf16[1,48,1500]{2,1,0:T(8,128)(2,1)S(1)}, bf16[1,48,1500]{2,1,0:T(8,128)(2,1)S(1)}) custom-call(s32[4]{0:T(128)S(1)} %get-tuple-element.66.offsets, bf16[1500,1024]{1,0:T(8,128)(2,1)S(1)} %get-tuple-element.67.chol.refs_8_), custom_call_target="tpu_custom_call" | custom-call | bytes 3072016 | tf_op jit(solution)/shard_map/cond/branch_1_fun/pallas_call | solution.py:145
  19.9 0.1 collective-permute-start.29
  19.9 1.4 %collective-permute-done.29 = bf16[1,48,1500]{2,1,0:T(8,128)(2,1)S(1)} collective-permute-done((bf16[1,48,1500]{2,1,0:T(8,128)(2,1)S(1)}, bf16[1,48,1500]{2,1,0:T(8,128)(2,1)S(1)}, u32[]{:S(2)}, u32[]{:S(2)}) %collective-permute-start.29) | collective-permute-done | bytes 144032 | tf_op jit(solution)/shard_map/cond/branch_1_fun/ppermute | solution.py:178
  21.3 6.7 %collective-permute-done.30.refs_2_ = bf16[1,80,1500]{2,1,0:T(8,128)(2,1)S(1)} collective-permute-done((bf16[1,80,1500]{2,1,0:T(8,128)(2,1)S(1)}, bf16[1,80,1500]{2,1,0:T(8,128)(2,1)S(1)}, u32[]{:S(2)}, u32[]{:S(2)}) %collective-permute-start.30) | collective-permute-done | bytes 240032 | tf_op jit(solution)/shard_map/cond/branch_1_fun/ppermute | solution.py:182
  28.1 0.5 collective-permute-start.33
  28.6 0.5 collective-permute-start.35
  29.1 0.5 collective-permute-done.32.refs_4_
  29.6 0.4 collective-permute-done.33.refs_5_
  29.9 0.4 collective-permute-done.34.refs_6_
  30.3 0.4 collective-permute-done.35.refs_7_
  30.6 2.4 %branch_1_fun.11.own = f32[336,1024]{1,0:T(8,128)S(1)} custom-call(s32[4]{0:T(128)S(1)} %get-tuple-element.66.offsets, bf16[1,80,1500]{2,1,0:T(8,128)(2,1)S(1)} %add.11.refs_0_, bf16[1,80,1500]{2,1,0:T(8,128)(2,1)S(1)} %collective-permute-done.28.refs_1_, bf16[1,80,1500]{2,1,0:T(8,128)(2,1)S(1)} %collective-permute-done.30.refs_2_, ...), custom_call_target="tpu_custom_call" | custom-call | flops 983040000 | bytes 4992016 | tf_op jit(solution)/shard_map/cond/branch_1_fun/pallas_call | solution.py:145
  33.0 0.1 convert_element_type.44
  33.1 1.6 %collective-permute-start.36 = (f16[336,1024]{1,0:T(8,128)(2,1)S(1)}, f16[336,1024]{1,0:T(8,128)(2,1)S(1)}, u32[]{:S(2)}, u32[]{:S(2)}) collective-permute-start(f16[336,1024]{1,0:T(8,128)(2,1)S(1)} %convert_element_type.44), channel_id=1, source_target_pairs={{0,8},{1,17},{2,10},{3,19},{4,12},{5,21},{6,14},{7,23},{8,0},{9,25... | collective-permute-start | bytes 2064392 | tf_op jit(solution)/shard_map/cond/branch_1_fun/ppermute | solution.py:200
  34.7 2.5 %collective-permute-start.37 = (bf16[1,48,1500]{2,1,0:T(8,128)(2,1)S(1)}, bf16[1,48,1500]{2,1,0:T(8,128)(2,1)S(1)}, u32[]{:S(2)}, u32[]{:S(2)}) collective-permute-start(bf16[1,48,1500]{2,1,0:T(8,128)(2,1)S(1)} %add.12.refs_0_), channel_id=1, source_target_pairs={{0,6},{1,7},{2,4},{3,5},{4,2},{5,3},{6,0},{7,1},{8,14},{9,15},{10,... | collective-permute-start | bytes 432008 | tf_op jit(solution)/shard_map/cond/branch_1_fun/ppermute | solution.py:182
  37.1 7.0 %collective-permute-done.36 = f16[336,1024]{1,0:T(8,128)(2,1)S(1)} collective-permute-done((f16[336,1024]{1,0:T(8,128)(2,1)S(1)}, f16[336,1024]{1,0:T(8,128)(2,1)S(1)}, u32[]{:S(2)}, u32[]{:S(2)}) %collective-permute-start.36) | collective-permute-done | bytes 688160 | tf_op jit(solution)/shard_map/cond/branch_1_fun/ppermute | solution.py:200
  44.1 0.1 convert_element_type.45.came
  44.2 0.2 branch_1_fun.12.own
  44.4 0.1 convert_element_type.46
  44.5 1.6 %collective-permute-start.40 = (f16[336,1024]{1,0:T(8,128)(2,1)S(1)}, f16[336,1024]{1,0:T(8,128)(2,1)S(1)}, u32[]{:S(2)}, u32[]{:S(2)}) collective-permute-start(f16[336,1024]{1,0:T(8,128)(2,1)S(1)} %convert_element_type.46), channel_id=1, source_target_pairs={{0,16},{1,9},{2,18},{3,11},{4,20},{5,13},{6,22},{7,15},{8,24},{9,1... | collective-permute-start | bytes 2064392 | tf_op jit(solution)/shard_map/cond/branch_1_fun/ppermute | solution.py:200
  46.1 4.8 %collective-permute-start.38 = (bf16[1,48,1500]{2,1,0:T(8,128)(2,1)S(1)}, bf16[1,48,1500]{2,1,0:T(8,128)(2,1)S(1)}, u32[]{:S(2)}, u32[]{:S(2)}) collective-permute-start(bf16[1,48,1500]{2,1,0:T(8,128)(2,1)S(1)} %add.12.refs_0_), channel_id=1, source_target_pairs={{0,2},{1,3},{2,0},{3,1},{4,6},{5,7},{6,4},{7,5},{8,10},{9,11},{10,... | collective-permute-start | bytes 432008 | tf_op jit(solution)/shard_map/cond/branch_1_fun/ppermute | solution.py:182
  50.9 1.0 %collective-permute-start.39 = (bf16[1,48,1500]{2,1,0:T(8,128)(2,1)S(1)}, bf16[1,48,1500]{2,1,0:T(8,128)(2,1)S(1)}, u32[]{:S(2)}, u32[]{:S(2)}) collective-permute-start(bf16[1,48,1500]{2,1,0:T(8,128)(2,1)S(1)} %add.12.refs_0_), channel_id=1, source_target_pairs={{0,4},{1,5},{2,6},{3,7},{4,0},{5,1},{6,2},{7,3},{8,12},{9,13},{10,... | collective-permute-start | bytes 432008 | tf_op jit(solution)/shard_map/cond/branch_1_fun/ppermute | solution.py:182
  51.9 3.7 %collective-permute-done.40 = f16[336,1024]{1,0:T(8,128)(2,1)S(1)} collective-permute-done((f16[336,1024]{1,0:T(8,128)(2,1)S(1)}, f16[336,1024]{1,0:T(8,128)(2,1)S(1)}, u32[]{:S(2)}, u32[]{:S(2)}) %collective-permute-start.40) | collective-permute-done | bytes 688160 | tf_op jit(solution)/shard_map/cond/branch_1_fun/ppermute | solution.py:200
  55.5 0.1 convert_element_type.47.came
  55.6 1.0 %branch_1_fun.13 = (f32[4,40,1024]{2,1,0:T(8,128)S(1)}, f32[4,40,1024]{2,1,0:T(8,128)S(1)}) custom-call(f32[336,1024]{1,0:T(8,128)S(1)} %branch_1_fun.12.own, f32[336,1024]{1,0:T(8,128)S(1)} %convert_element_type.47.came, bf16[1024,1024]{1,0:T(8,128)(2,1)S(1)} %copy-done.2), custom_call_target="tpu_custom_call" | custom-call | flops 671088640 | bytes 4849664 | tf_op jit(solution)/shard_map/cond/branch_1_fun/pallas_call | solution.py:145
  56.7 0.1 collective-permute-start.46
  56.8 2.7 %collective-permute-done.39.refs_2_ = bf16[1,48,1500]{2,1,0:T(8,128)(2,1)S(1)} collective-permute-done((bf16[1,48,1500]{2,1,0:T(8,128)(2,1)S(1)}, bf16[1,48,1500]{2,1,0:T(8,128)(2,1)S(1)}, u32[]{:S(2)}, u32[]{:S(2)}) %collective-permute-start.39) | collective-permute-done | bytes 144032 | tf_op jit(solution)/shard_map/cond/branch_1_fun/ppermute | solution.py:182
  59.4 0.5 collective-permute-start.42
  59.9 0.5 collective-permute-start.44
  60.4 0.3 collective-permute-done.41.refs_4_
  60.8 0.2 collective-permute-done.42.refs_5_
  61.0 0.3 collective-permute-done.43.refs_6_
  61.3 0.2 collective-permute-done.44.refs_7_
  61.5 1.7 %branch_1_fun.14.own = f32[208,1024]{1,0:T(8,128)S(1)} custom-call(s32[4]{0:T(128)S(1)} %get-tuple-element.66.offsets, bf16[1,48,1500]{2,1,0:T(8,128)(2,1)S(1)} %add.12.refs_0_, bf16[1,48,1500]{2,1,0:T(8,128)(2,1)S(1)} %collective-permute-done.38.refs_1_, bf16[1,48,1500]{2,1,0:T(8,128)(2,1)S(1)} %collective-permute-done.39.refs_2_, ...), custom_call_target="tpu_custom_call" | custom-call | flops 589824000 | bytes 4224016 | tf_op jit(solution)/shard_map/cond/branch_1_fun/pallas_call | solution.py:145
  63.2 0.1 convert_element_type.48
  63.3 0.6 collective-permute-start.45
  63.9 0.1 branch_1_fun.16
  64.0 3.9 %collective-permute-start.47 = (bf16[40,1024]{1,0:T(8,128)(2,1)S(1)}, bf16[40,1024]{1,0:T(8,128)(2,1)S(1)}, u32[]{:S(2)}, u32[]{:S(2)}) collective-permute-start(bf16[40,1024]{1,0:T(8,128)(2,1)S(1)} %get-tuple-element.87), channel_id=1, source_target_pairs={{0,2},{1,3},{2,0},{3,1},{4,6},{5,7},{6,4},{7,5},{8,10},{9,11},{10,... | collective-permute-start | bytes 245768 | tf_op jit(solution)/shard_map/cond/branch_1_fun/ppermute | solution.py:231
  67.9 1.1 %collective-permute-start.48 = (bf16[40,1024]{1,0:T(8,128)(2,1)S(1)}, bf16[40,1024]{1,0:T(8,128)(2,1)S(1)}, u32[]{:S(2)}, u32[]{:S(2)}) collective-permute-start(bf16[40,1024]{1,0:T(8,128)(2,1)S(1)} %get-tuple-element.88), channel_id=1, source_target_pairs={{0,4},{1,5},{2,6},{3,7},{4,0},{5,1},{6,2},{7,3},{8,12},{9,13},{10,... | collective-permute-start | bytes 245768 | tf_op jit(solution)/shard_map/cond/branch_1_fun/ppermute | solution.py:231
  69.0 1.4 %collective-permute-start.49 = (bf16[40,1024]{1,0:T(8,128)(2,1)S(1)}, bf16[40,1024]{1,0:T(8,128)(2,1)S(1)}, u32[]{:S(2)}, u32[]{:S(2)}) collective-permute-start(bf16[40,1024]{1,0:T(8,128)(2,1)S(1)} %get-tuple-element.89), channel_id=1, source_target_pairs={{0,6},{1,7},{2,4},{3,5},{4,2},{5,3},{6,0},{7,1},{8,14},{9,15},{10,... | collective-permute-start | bytes 245768 | tf_op jit(solution)/shard_map/cond/branch_1_fun/ppermute | solution.py:231
  70.4 1.1 %collective-permute-done.45 = f16[208,1024]{1,0:T(8,128)(2,1)S(1)} collective-permute-done((f16[208,1024]{1,0:T(8,128)(2,1)S(1)}, f16[208,1024]{1,0:T(8,128)(2,1)S(1)}, u32[]{:S(2)}, u32[]{:S(2)}) %collective-permute-start.45) | collective-permute-done | bytes 426016 | tf_op jit(solution)/shard_map/cond/branch_1_fun/ppermute | solution.py:200
  71.5 0.1 convert_element_type.49.came
  71.6 0.1 branch_1_fun.15.own
  71.7 5.5 %collective-permute-done.48.refs_2_ = bf16[40,1024]{1,0:T(8,128)(2,1)S(1)} collective-permute-done((bf16[40,1024]{1,0:T(8,128)(2,1)S(1)}, bf16[40,1024]{1,0:T(8,128)(2,1)S(1)}, u32[]{:S(2)}, u32[]{:S(2)}) %collective-permute-start.48) | collective-permute-done | bytes 81952 | tf_op jit(solution)/shard_map/cond/branch_1_fun/ppermute | solution.py:231
  77.1 0.1 convert_element_type.50
  77.2 0.6 collective-permute-start.50
  77.8 7.6 %collective-permute-done.50 = f16[208,1024]{1,0:T(8,128)(2,1)S(1)} collective-permute-done((f16[208,1024]{1,0:T(8,128)(2,1)S(1)}, f16[208,1024]{1,0:T(8,128)(2,1)S(1)}, u32[]{:S(2)}, u32[]{:S(2)}) %collective-permute-start.50) | collective-permute-done | bytes 426016 | tf_op jit(solution)/shard_map/cond/branch_1_fun/ppermute | solution.py:200
  85.4 0.1 convert_element_type.51.came
  85.5 0.7 branch_1_fun.17
  86.2 0.1 collective-permute-start.51
  86.3 1.7 %collective-permute-done.51.came = f32[4,24,1024]{2,1,0:T(8,128)S(1)} collective-permute-done((f32[4,24,1024]{2,1,0:T(8,128)S(1)}, f32[4,24,1024]{2,1,0:T(8,128)S(1)}, u32[]{:S(2)}, u32[]{:S(2)}) %collective-permute-start.51) | collective-permute-done | bytes 393248 | tf_op jit(solution)/shard_map/cond/branch_1_fun/ppermute | solution.py:258
  88.0 1.5 %collective-permute-start.52 = (bf16[24,1024]{1,0:T(8,128)(2,1)S(1)}, bf16[24,1024]{1,0:T(8,128)(2,1)S(1)}, u32[]{:S(2)}, u32[]{:S(2)}) collective-permute-start(bf16[24,1024]{1,0:T(8,128)(2,1)S(1)} %get-tuple-element.98), channel_id=1, source_target_pairs={{0,2},{1,3},{2,0},{3,1},{4,6},{5,7},{6,4},{7,5},{8,10},{9,11},{10,... | collective-permute-start | bytes 147464 | tf_op jit(solution)/shard_map/cond/branch_1_fun/ppermute | solution.py:231
  89.5 1.3 %collective-permute-start.53 = (bf16[24,1024]{1,0:T(8,128)(2,1)S(1)}, bf16[24,1024]{1,0:T(8,128)(2,1)S(1)}, u32[]{:S(2)}, u32[]{:S(2)}) collective-permute-start(bf16[24,1024]{1,0:T(8,128)(2,1)S(1)} %get-tuple-element.99), channel_id=1, source_target_pairs={{0,4},{1,5},{2,6},{3,7},{4,0},{5,1},{6,2},{7,3},{8,12},{9,13},{10,... | collective-permute-start | bytes 147464 | tf_op jit(solution)/shard_map/cond/branch_1_fun/ppermute | solution.py:231
  90.9 1.6 %collective-permute-start.54 = (bf16[24,1024]{1,0:T(8,128)(2,1)S(1)}, bf16[24,1024]{1,0:T(8,128)(2,1)S(1)}, u32[]{:S(2)}, u32[]{:S(2)}) collective-permute-start(bf16[24,1024]{1,0:T(8,128)(2,1)S(1)} %get-tuple-element.100), channel_id=1, source_target_pairs={{0,6},{1,7},{2,4},{3,5},{4,2},{5,3},{6,0},{7,1},{8,14},{9,15},{10,... | collective-permute-start | bytes 147464 | tf_op jit(solution)/shard_map/cond/branch_1_fun/ppermute | solution.py:231
  92.5 3.5 %collective-permute-done.53.refs_6_ = bf16[24,1024]{1,0:T(8,128)(2,1)S(1)} collective-permute-done((bf16[24,1024]{1,0:T(8,128)(2,1)S(1)}, bf16[24,1024]{1,0:T(8,128)(2,1)S(1)}, u32[]{:S(2)}, u32[]{:S(2)}) %collective-permute-start.53) | collective-permute-done | bytes 49184 | tf_op jit(solution)/shard_map/cond/branch_1_fun/ppermute | solution.py:231
  96.0 0.8 collective-permute-done.54.refs_7_
  97.2 0.7 copy-done.3
  (22 shorter events, 0.2 us)
Async XLA Ops:
  0.0 4.7 %copy-start = (bf16[1500,1024]{1,0:T(8,128)(2,1)S(1)}, bf16[1500,1024]{1,0:T(8,128)(2,1)}, u32[]{:S(2)}) copy-start(bf16[1500,1024]{1,0:T(8,128)(2,1)} %chol.1) | copy-start | bytes 9216004
  0.0 4.7 %copy-start.4 = (s32[4]{0:T(128)S(1)}, s32[4]{0:T(128)}, u32[]{:S(2)}) copy-start(s32[4]{0:T(128)} %offsets.1) | copy-start | bytes 52
  3.0 1.7 %collective-permute-start.55 = (bf16[1,80,1500]{2,1,0:T(8,128)(2,1)S(1)}, bf16[1,80,1500]{2,1,0:T(8,128)(2,1)S(1)}, u32[]{:S(2)}, u32[]{:S(2)}) collective-permute-start(bf16[1,80,1500]{2,1,0:T(8,128)(2,1)S(1)} %get-tuple-element.106), channel_id=1, source_target_pairs={{0,1},{1,0},{2,3},{3,2},{4,5},{5,4},{6,7},{7,6},{8,9},{9,8},{10,11... | collective-permute-start | bytes 720008 | tf_op jit(solution)/shard_map/ppermute | solution.py:178
  4.8 13.9 %collective-permute-start.28 = (bf16[1,80,1500]{2,1,0:T(8,128)(2,1)S(1)}, bf16[1,80,1500]{2,1,0:T(8,128)(2,1)S(1)}, u32[]{:S(2)}, u32[]{:S(2)}) collective-permute-start(bf16[1,80,1500]{2,1,0:T(8,128)(2,1)S(1)} %add.11.refs_0_), channel_id=1, source_target_pairs={{0,2},{1,3},{2,0},{3,1},{4,6},{5,7},{6,4},{7,5},{8,10},{9,11},{10,... | collective-permute-start | bytes 720008 | tf_op jit(solution)/shard_map/cond/branch_1_fun/ppermute | solution.py:182
  7.8 20.3 %collective-permute-start.30 = (bf16[1,80,1500]{2,1,0:T(8,128)(2,1)S(1)}, bf16[1,80,1500]{2,1,0:T(8,128)(2,1)S(1)}, u32[]{:S(2)}, u32[]{:S(2)}) collective-permute-start(bf16[1,80,1500]{2,1,0:T(8,128)(2,1)S(1)} %add.11.refs_0_), channel_id=1, source_target_pairs={{0,4},{1,5},{2,6},{3,7},{4,0},{5,1},{6,2},{7,3},{8,12},{9,13},{10,... | collective-permute-start | bytes 720008 | tf_op jit(solution)/shard_map/cond/branch_1_fun/ppermute | solution.py:182
  10.4 17.7 %collective-permute-start.31 = (bf16[1,80,1500]{2,1,0:T(8,128)(2,1)S(1)}, bf16[1,80,1500]{2,1,0:T(8,128)(2,1)S(1)}, u32[]{:S(2)}, u32[]{:S(2)}) collective-permute-start(bf16[1,80,1500]{2,1,0:T(8,128)(2,1)S(1)} %add.11.refs_0_), channel_id=1, source_target_pairs={{0,6},{1,7},{2,4},{3,5},{4,2},{5,3},{6,0},{7,1},{8,14},{9,15},{10,... | collective-permute-start | bytes 720008 | tf_op jit(solution)/shard_map/cond/branch_1_fun/ppermute | solution.py:182
  19.9 1.4 %collective-permute-start.29 = (bf16[1,48,1500]{2,1,0:T(8,128)(2,1)S(1)}, bf16[1,48,1500]{2,1,0:T(8,128)(2,1)S(1)}, u32[]{:S(2)}, u32[]{:S(2)}) collective-permute-start(bf16[1,48,1500]{2,1,0:T(8,128)(2,1)S(1)} %get-tuple-element.69), channel_id=1, source_target_pairs={{0,1},{1,0},{2,3},{3,2},{4,5},{5,4},{6,7},{7,6},{8,9},{9,8},{10,11... | collective-permute-start | bytes 432008 | tf_op jit(solution)/shard_map/cond/branch_1_fun/ppermute | solution.py:178
  28.1 1.5 %collective-permute-start.32 = (bf16[1,80,1500]{2,1,0:T(8,128)(2,1)S(1)}, bf16[1,80,1500]{2,1,0:T(8,128)(2,1)S(1)}, u32[]{:S(2)}, u32[]{:S(2)}) collective-permute-start(bf16[1,80,1500]{2,1,0:T(8,128)(2,1)S(1)} %add.11.refs_0_), channel_id=1, source_target_pairs={{0,1},{1,0},{2,3},{3,2},{4,5},{5,4},{6,7},{7,6},{8,9},{9,8},{10,11... | collective-permute-start | bytes 720008 | tf_op jit(solution)/shard_map/cond/branch_1_fun/ppermute | solution.py:186
  28.1 1.9 %collective-permute-start.33 = (bf16[1,80,1500]{2,1,0:T(8,128)(2,1)S(1)}, bf16[1,80,1500]{2,1,0:T(8,128)(2,1)S(1)}, u32[]{:S(2)}, u32[]{:S(2)}) collective-permute-start(bf16[1,80,1500]{2,1,0:T(8,128)(2,1)S(1)} %collective-permute-done.28.refs_1_), channel_id=1, source_target_pairs={{0,1},{1,0},{2,3},{3,2},{4,5},{5,4},{6,7},{7,6},{8,9},{9,8},{10,11... | collective-permute-start | bytes 720008 | tf_op jit(solution)/shard_map/cond/branch_1_fun/ppermute | solution.py:186
  28.6 1.7 %collective-permute-start.34 = (bf16[1,80,1500]{2,1,0:T(8,128)(2,1)S(1)}, bf16[1,80,1500]{2,1,0:T(8,128)(2,1)S(1)}, u32[]{:S(2)}, u32[]{:S(2)}) collective-permute-start(bf16[1,80,1500]{2,1,0:T(8,128)(2,1)S(1)} %collective-permute-done.30.refs_2_), channel_id=1, source_target_pairs={{0,1},{1,0},{2,3},{3,2},{4,5},{5,4},{6,7},{7,6},{8,9},{9,8},{10,11... | collective-permute-start | bytes 720008 | tf_op jit(solution)/shard_map/cond/branch_1_fun/ppermute | solution.py:186
  28.6 2.1 %collective-permute-start.35 = (bf16[1,80,1500]{2,1,0:T(8,128)(2,1)S(1)}, bf16[1,80,1500]{2,1,0:T(8,128)(2,1)S(1)}, u32[]{:S(2)}, u32[]{:S(2)}) collective-permute-start(bf16[1,80,1500]{2,1,0:T(8,128)(2,1)S(1)} %collective-permute-done.31.refs_3_), channel_id=1, source_target_pairs={{0,1},{1,0},{2,3},{3,2},{4,5},{5,4},{6,7},{7,6},{8,9},{9,8},{10,11... | collective-permute-start | bytes 720008 | tf_op jit(solution)/shard_map/cond/branch_1_fun/ppermute | solution.py:186
  33.1 11.0 %collective-permute-start.36 = (f16[336,1024]{1,0:T(8,128)(2,1)S(1)}, f16[336,1024]{1,0:T(8,128)(2,1)S(1)}, u32[]{:S(2)}, u32[]{:S(2)}) collective-permute-start(f16[336,1024]{1,0:T(8,128)(2,1)S(1)} %convert_element_type.44), channel_id=1, source_target_pairs={{0,8},{1,17},{2,10},{3,19},{4,12},{5,21},{6,14},{7,23},{8,0},{9,25... | collective-permute-start | bytes 2064392 | tf_op jit(solution)/shard_map/cond/branch_1_fun/ppermute | solution.py:200
  34.7 9.6 %collective-permute-start.37 = (bf16[1,48,1500]{2,1,0:T(8,128)(2,1)S(1)}, bf16[1,48,1500]{2,1,0:T(8,128)(2,1)S(1)}, u32[]{:S(2)}, u32[]{:S(2)}) collective-permute-start(bf16[1,48,1500]{2,1,0:T(8,128)(2,1)S(1)} %add.12.refs_0_), channel_id=1, source_target_pairs={{0,6},{1,7},{2,4},{3,5},{4,2},{5,3},{6,0},{7,1},{8,14},{9,15},{10,... | collective-permute-start | bytes 432008 | tf_op jit(solution)/shard_map/cond/branch_1_fun/ppermute | solution.py:182
  44.4 11.2 %copy-start.2 = (bf16[1024,1024]{1,0:T(8,128)(2,1)S(1)}, bf16[1024,1024]{1,0:T(8,128)(2,1)}, u32[]{:S(2)}) copy-start(bf16[1024,1024]{1,0:T(8,128)(2,1)} %get-tuple-element.78.amplitudes) | copy-start | bytes 6291460 | tf_op jit(solution)/shard_map/cond
  44.5 11.0 %collective-permute-start.40 = (f16[336,1024]{1,0:T(8,128)(2,1)S(1)}, f16[336,1024]{1,0:T(8,128)(2,1)S(1)}, u32[]{:S(2)}, u32[]{:S(2)}) collective-permute-start(f16[336,1024]{1,0:T(8,128)(2,1)S(1)} %convert_element_type.46), channel_id=1, source_target_pairs={{0,16},{1,9},{2,18},{3,11},{4,20},{5,13},{6,22},{7,15},{8,24},{9,1... | collective-permute-start | bytes 2064392 | tf_op jit(solution)/shard_map/cond/branch_1_fun/ppermute | solution.py:200
  46.1 10.6 %collective-permute-start.38 = (bf16[1,48,1500]{2,1,0:T(8,128)(2,1)S(1)}, bf16[1,48,1500]{2,1,0:T(8,128)(2,1)S(1)}, u32[]{:S(2)}, u32[]{:S(2)}) collective-permute-start(bf16[1,48,1500]{2,1,0:T(8,128)(2,1)S(1)} %add.12.refs_0_), channel_id=1, source_target_pairs={{0,2},{1,3},{2,0},{3,1},{4,6},{5,7},{6,4},{7,5},{8,10},{9,11},{10,... | collective-permute-start | bytes 432008 | tf_op jit(solution)/shard_map/cond/branch_1_fun/ppermute | solution.py:182
  50.9 8.6 %collective-permute-start.39 = (bf16[1,48,1500]{2,1,0:T(8,128)(2,1)S(1)}, bf16[1,48,1500]{2,1,0:T(8,128)(2,1)S(1)}, u32[]{:S(2)}, u32[]{:S(2)}) collective-permute-start(bf16[1,48,1500]{2,1,0:T(8,128)(2,1)S(1)} %add.12.refs_0_), channel_id=1, source_target_pairs={{0,4},{1,5},{2,6},{3,7},{4,0},{5,1},{6,2},{7,3},{8,12},{9,13},{10,... | collective-permute-start | bytes 432008 | tf_op jit(solution)/shard_map/cond/branch_1_fun/ppermute | solution.py:182
  56.7 7.3 %collective-permute-start.46 = (f32[4,40,1024]{2,1,0:T(8,128)S(1)}, f32[4,40,1024]{2,1,0:T(8,128)S(1)}, u32[]{:S(2)}, u32[]{:S(2)}) collective-permute-start(f32[4,40,1024]{2,1,0:T(8,128)S(1)} %get-tuple-element.79), channel_id=1, source_target_pairs={{0,1},{1,0},{2,3},{3,2},{4,5},{5,4},{6,7},{7,6},{8,9},{9,8},{10,11... | collective-permute-start | bytes 1966088 | tf_op jit(solution)/shard_map/cond/branch_1_fun/ppermute | solution.py:247
  59.4 1.4 %collective-permute-start.41 = (bf16[1,48,1500]{2,1,0:T(8,128)(2,1)S(1)}, bf16[1,48,1500]{2,1,0:T(8,128)(2,1)S(1)}, u32[]{:S(2)}, u32[]{:S(2)}) collective-permute-start(bf16[1,48,1500]{2,1,0:T(8,128)(2,1)S(1)} %add.12.refs_0_), channel_id=1, source_target_pairs={{0,1},{1,0},{2,3},{3,2},{4,5},{5,4},{6,7},{7,6},{8,9},{9,8},{10,11... | collective-permute-start | bytes 432008 | tf_op jit(solution)/shard_map/cond/branch_1_fun/ppermute | solution.py:186
  59.4 1.6 %collective-permute-start.42 = (bf16[1,48,1500]{2,1,0:T(8,128)(2,1)S(1)}, bf16[1,48,1500]{2,1,0:T(8,128)(2,1)S(1)}, u32[]{:S(2)}, u32[]{:S(2)}) collective-permute-start(bf16[1,48,1500]{2,1,0:T(8,128)(2,1)S(1)} %collective-permute-done.38.refs_1_), channel_id=1, source_target_pairs={{0,1},{1,0},{2,3},{3,2},{4,5},{5,4},{6,7},{7,6},{8,9},{9,8},{10,11... | collective-permute-start | bytes 432008 | tf_op jit(solution)/shard_map/cond/branch_1_fun/ppermute | solution.py:186
  59.9 1.4 %collective-permute-start.43 = (bf16[1,48,1500]{2,1,0:T(8,128)(2,1)S(1)}, bf16[1,48,1500]{2,1,0:T(8,128)(2,1)S(1)}, u32[]{:S(2)}, u32[]{:S(2)}) collective-permute-start(bf16[1,48,1500]{2,1,0:T(8,128)(2,1)S(1)} %collective-permute-done.39.refs_2_), channel_id=1, source_target_pairs={{0,1},{1,0},{2,3},{3,2},{4,5},{5,4},{6,7},{7,6},{8,9},{9,8},{10,11... | collective-permute-start | bytes 432008 | tf_op jit(solution)/shard_map/cond/branch_1_fun/ppermute | solution.py:186
  59.9 1.6 %collective-permute-start.44 = (bf16[1,48,1500]{2,1,0:T(8,128)(2,1)S(1)}, bf16[1,48,1500]{2,1,0:T(8,128)(2,1)S(1)}, u32[]{:S(2)}, u32[]{:S(2)}) collective-permute-start(bf16[1,48,1500]{2,1,0:T(8,128)(2,1)S(1)} %collective-permute-done.37.refs_3_), channel_id=1, source_target_pairs={{0,1},{1,0},{2,3},{3,2},{4,5},{5,4},{6,7},{7,6},{8,9},{9,8},{10,11... | collective-permute-start | bytes 432008 | tf_op jit(solution)/shard_map/cond/branch_1_fun/ppermute | solution.py:186
  63.3 8.2 %collective-permute-start.45 = (f16[208,1024]{1,0:T(8,128)(2,1)S(1)}, f16[208,1024]{1,0:T(8,128)(2,1)S(1)}, u32[]{:S(2)}, u32[]{:S(2)}) collective-permute-start(f16[208,1024]{1,0:T(8,128)(2,1)S(1)} %convert_element_type.48), channel_id=1, source_target_pairs={{0,8},{1,17},{2,10},{3,19},{4,12},{5,21},{6,14},{7,23},{8,0},{9,25... | collective-permute-start | bytes 1277960 | tf_op jit(solution)/shard_map/cond/branch_1_fun/ppermute | solution.py:200
  64.0 7.7 %collective-permute-start.47 = (bf16[40,1024]{1,0:T(8,128)(2,1)S(1)}, bf16[40,1024]{1,0:T(8,128)(2,1)S(1)}, u32[]{:S(2)}, u32[]{:S(2)}) collective-permute-start(bf16[40,1024]{1,0:T(8,128)(2,1)S(1)} %get-tuple-element.87), channel_id=1, source_target_pairs={{0,2},{1,3},{2,0},{3,1},{4,6},{5,7},{6,4},{7,5},{8,10},{9,11},{10,... | collective-permute-start | bytes 245768 | tf_op jit(solution)/shard_map/cond/branch_1_fun/ppermute | solution.py:231
  67.9 9.2 %collective-permute-start.48 = (bf16[40,1024]{1,0:T(8,128)(2,1)S(1)}, bf16[40,1024]{1,0:T(8,128)(2,1)S(1)}, u32[]{:S(2)}, u32[]{:S(2)}) collective-permute-start(bf16[40,1024]{1,0:T(8,128)(2,1)S(1)} %get-tuple-element.88), channel_id=1, source_target_pairs={{0,4},{1,5},{2,6},{3,7},{4,0},{5,1},{6,2},{7,3},{8,12},{9,13},{10,... | collective-permute-start | bytes 245768 | tf_op jit(solution)/shard_map/cond/branch_1_fun/ppermute | solution.py:231
  69.0 8.2 %collective-permute-start.49 = (bf16[40,1024]{1,0:T(8,128)(2,1)S(1)}, bf16[40,1024]{1,0:T(8,128)(2,1)S(1)}, u32[]{:S(2)}, u32[]{:S(2)}) collective-permute-start(bf16[40,1024]{1,0:T(8,128)(2,1)S(1)} %get-tuple-element.89), channel_id=1, source_target_pairs={{0,6},{1,7},{2,4},{3,5},{4,2},{5,3},{6,0},{7,1},{8,14},{9,15},{10,... | collective-permute-start | bytes 245768 | tf_op jit(solution)/shard_map/cond/branch_1_fun/ppermute | solution.py:231
  77.2 8.2 %collective-permute-start.50 = (f16[208,1024]{1,0:T(8,128)(2,1)S(1)}, f16[208,1024]{1,0:T(8,128)(2,1)S(1)}, u32[]{:S(2)}, u32[]{:S(2)}) collective-permute-start(f16[208,1024]{1,0:T(8,128)(2,1)S(1)} %convert_element_type.50), channel_id=1, source_target_pairs={{0,16},{1,9},{2,18},{3,11},{4,20},{5,13},{6,22},{7,15},{8,24},{9,1... | collective-permute-start | bytes 1277960 | tf_op jit(solution)/shard_map/cond/branch_1_fun/ppermute | solution.py:200
  86.2 1.8 %collective-permute-start.51 = (f32[4,24,1024]{2,1,0:T(8,128)S(1)}, f32[4,24,1024]{2,1,0:T(8,128)S(1)}, u32[]{:S(2)}, u32[]{:S(2)}) collective-permute-start(f32[4,24,1024]{2,1,0:T(8,128)S(1)} %get-tuple-element.96), channel_id=1, source_target_pairs={{0,1},{1,0},{2,3},{3,2},{4,5},{5,4},{6,7},{7,6},{8,9},{9,8},{10,11... | collective-permute-start | bytes 1179656 | tf_op jit(solution)/shard_map/cond/branch_1_fun/ppermute | solution.py:258
  88.0 4.5 %collective-permute-start.52 = (bf16[24,1024]{1,0:T(8,128)(2,1)S(1)}, bf16[24,1024]{1,0:T(8,128)(2,1)S(1)}, u32[]{:S(2)}, u32[]{:S(2)}) collective-permute-start(bf16[24,1024]{1,0:T(8,128)(2,1)S(1)} %get-tuple-element.98), channel_id=1, source_target_pairs={{0,2},{1,3},{2,0},{3,1},{4,6},{5,7},{6,4},{7,5},{8,10},{9,11},{10,... | collective-permute-start | bytes 147464 | tf_op jit(solution)/shard_map/cond/branch_1_fun/ppermute | solution.py:231
  89.5 6.5 %collective-permute-start.53 = (bf16[24,1024]{1,0:T(8,128)(2,1)S(1)}, bf16[24,1024]{1,0:T(8,128)(2,1)S(1)}, u32[]{:S(2)}, u32[]{:S(2)}) collective-permute-start(bf16[24,1024]{1,0:T(8,128)(2,1)S(1)} %get-tuple-element.99), channel_id=1, source_target_pairs={{0,4},{1,5},{2,6},{3,7},{4,0},{5,1},{6,2},{7,3},{8,12},{9,13},{10,... | collective-permute-start | bytes 147464 | tf_op jit(solution)/shard_map/cond/branch_1_fun/ppermute | solution.py:231
  90.9 6.0 %collective-permute-start.54 = (bf16[24,1024]{1,0:T(8,128)(2,1)S(1)}, bf16[24,1024]{1,0:T(8,128)(2,1)S(1)}, u32[]{:S(2)}, u32[]{:S(2)}) collective-permute-start(bf16[24,1024]{1,0:T(8,128)(2,1)S(1)} %get-tuple-element.100), channel_id=1, source_target_pairs={{0,6},{1,7},{2,4},{3,5},{4,2},{5,3},{6,0},{7,1},{8,14},{9,15},{10,... | collective-permute-start | bytes 147464 | tf_op jit(solution)/shard_map/cond/branch_1_fun/ppermute | solution.py:231
  97.1 0.7 copy-start.3
where the time goes:
time: 98 us; the launch traced here: 97.8 us
  waiting for transfers between devices  53.1 us (54%)
  starting transfers between devices  31.8 us (32%)
  Pallas kernels  10.4 us (11%)
    ppermute x4, waiting for transfers between devices, swap(): came = lax.ppermute(block.astype(jnp.float16), AXES, in_plane[j])  19.4 us
    ppermute x6, waiting for transfers between devices, jump(): return lax.ppermute(own, AXES, jumps[j])  17.7 us
    ppermute x6, starting transfers between devices, jump(): return lax.ppermute(own, AXES, jumps[j])  13.8 us
    ppermute x6, starting transfers between devices, deliver(): return [lax.ppermute(g, AXES, jumps[j]) for j, g in enumerate(gives, 1)]  10.8 us
    pallas_call x11, Pallas kernels, call(): pl.pallas_call(kernel, out_shape=outs, out_specs=jax.tree.map(place, outs...  10.4 us
    ppermute x6, waiting for transfers between devices, deliver(): return [lax.ppermute(g, AXES, jumps[j]) for j, g in enumerate(gives, 1)]  9.85 us
    ppermute x4, starting transfers between devices, swap(): came = lax.ppermute(block.astype(jnp.float16), AXES, in_plane[j])  4.33 us
    ppermute x8, waiting for transfers between devices, integrals(): other = [lax.ppermute(m, AXES, swap_core) for m in mine]  2.61 us
  transfers between devices with their start and end apart: 28, of which 21 were waited for; matrix products, arithmetic and copies ran while one was open for 0% of the time, Pallas kernels for 4%

commit v1 on v0

--- a/solution.py
+++ b/solution.py
@@ -35,7 +35,8 @@
     return block, seen > index
 
 
-def pick_kernel(base, part, share, offsets, chol, keep, give, *most):
+def pick_kernel(base, part, share, offsets, chol, keep, give, *refs):
+    *most, held, done = refs
     cap, unit, depth = keep.shape
     width = chol.shape[1]
     col = lax.axis_index("col")
@@ -44,6 +45,7 @@
     t = lax.broadcasted_iota(jnp.int32, (unit, window), 0)
     lane = lax.broadcasted_iota(jnp.int32, (unit, window), 1)
     place = lax.div(t, part) * share + base + lax.rem(t, part)
+    jobs = []
     for slot in range(cap):
         for ref, parity in ((give, 1 - core), (keep, core)):
             block, there = entry(offsets, chip, width, 2 * slot + parity)
@@ -51,13 +53,16 @@
             left = jnp.clip(lax.shift_right_arithmetic(start, 7), 0, width // AB_TILE - 2)
             left = pl.multiple_of(left * AB_TILE, AB_TILE)
             start = jnp.where(there, start, -4 * AB_TILE - width)
-            hit = (lane + left == place + start).astype(jnp.float32).astype(jnp.bfloat16)
-            ref[slot] = lax.dot_general(
-                hit,
-                chol[:, pl.ds(left, window)],
-                (((1,), (1,)), ((), ())),
-                preferred_element_type=jnp.float32,
-            ).astype(jnp.bfloat16)
+            at = len(jobs)
+            copy = pltpu.make_async_copy(chol.at[:, pl.ds(left, window)], held.at[at], done.at[at])
+            copy.start()
+            jobs.append((copy, ref, slot, start - left))
+    for at, (copy, ref, slot, start) in enumerate(jobs):
+        hit = (lane == place + start).astype(jnp.float32).astype(jnp.bfloat16)
+        copy.wait()
+        ref[slot] = lax.dot_general(
+            hit, held[at], (((1,), (1,)), ((), ())), preferred_element_type=jnp.float32
+        ).astype(jnp.bfloat16)
     for ref in most:
         value = jnp.int32(0)
         for place in range(lax.axis_size("col") // 2):
@@ -139,7 +144,7 @@
         base += value.shape[0]
 
 
-def call(kernel, outs, smem, *args, scratch=(), flops=0):
+def call(kernel, outs, smem, *args, scratch=(), flops=0, memory=pltpu.VMEM):
     size = sum(a.size * a.dtype.itemsize for a in args)
     place = lambda o: pl.BlockSpec(memory_space=pltpu.SMEM if o.dtype == jnp.int32 else pltpu.VMEM)
     return pl.pallas_call(
@@ -147,7 +152,7 @@
         out_shape=outs,
         out_specs=jax.tree.map(place, outs),
         in_specs=[pl.BlockSpec(memory_space=pltpu.SMEM)] * smem
-        + [pl.BlockSpec(memory_space=pltpu.VMEM)] * (len(args) - smem),
+        + [pl.BlockSpec(memory_space=memory)] * (len(args) - smem),
         scratch_shapes=list(scratch),
         compiler_params=VMEM,
         cost_estimate=pl.CostEstimate(flops=flops, bytes_accessed=size, transcendentals=0),
@@ -174,16 +179,32 @@
         def picked(cap, h, offsets, most=()):
             held = jax.ShapeDtypeStruct((cap, AB_TILE // share * parts[h], depth), jnp.bfloat16)
             kernel = functools.partial(pick_kernel, sum(parts[:h]), parts[h], share)
-            keep, give, *most = call(kernel, (held, held, *most), 1, offsets, chol)
-            return (keep + lax.ppermute(give, AXES, swap_core), *most)
+            keep, give, *most = call(
+                kernel,
+                (held, held, *most),
+                1,
+                offsets,
+                chol,
+                scratch=[
+                    pltpu.VMEM((2 * cap, depth, 2 * AB_TILE), jnp.bfloat16),
+                    pltpu.SemaphoreType.DMA((2 * cap,)),
+                ],
+                memory=pl.ANY,
+            )
+            return (keep, give, *most)
+
+        def merged(keep, give):
+            return keep + lax.ppermute(give, AXES, swap_core)
 
         def rest(cap, own):
             def jump(own, j):
                 return lax.ppermute(own, AXES, jumps[j])
 
-            def integrals(mine):
+            def across(m):
+                return lax.ppermute(m, AXES, swap_core)
+
+            def integrals(mine, other):
                 height = blocks * mine[0].shape[1]
-                other = [lax.ppermute(m, AXES, swap_core) for m in mine]
                 return call(
                     functools.partial(integrals_kernel, places),
                     jax.ShapeDtypeStruct((height + PAD, width), jnp.float32),
@@ -231,31 +252,34 @@
                 return [lax.ppermute(g, AXES, jumps[j]) for j, g in enumerate(gives, 1)]
 
             after = lax.optimization_barrier
-            mine = [own] + [jump(own, j) for j in range(1, places)]
-            offsets, _ = after((pair_offsets, mine[1]))
-            (own,) = picked(cap, 1, offsets)
-            own, *mine = after((own, *mine))
-            block = integrals(mine)
-            far = jump(own, places - 1)
+            two, one = after((jump(own, 2), jump(own, 1)))
+            three = jump(two, 1)
+            offsets, _ = after((pair_offsets, (one, two)))
+            keep, give = picked(cap, 1, offsets)
+            mine = [own, one, two]
+            other = [across(m) for m in mine]
+            own = merged(keep, give)
+            own, three, *other = after((own, three, *other))
+            block = integrals([*mine, three], [*other, across(three)])
+            two, one = jump(own, 2), jump(own, 1)
             came = swap(block, 0)
-            came, far = after((came, far))
+            came, two, one = after((came, two, one))
             block = join(block, came)
-            near, _ = after((own, block))
-            near = [jump(near, j) for j in range(1, places - 1)]
+            two, _ = after((two, block))
+            three = jump(two, 1)
             came = swap(block, 1)
+            mine = [own, one, two]
+            second = integrals([*mine, three], [across(m) for m in [*mine, three]])
+            second, came = after((second, came))
             keep, give = residual(block, came, parts[0])
-            got = lax.ppermute(give, AXES, swap_core)
-            own, far, *near, _ = after((own, far, *near, give))
-            second = integrals([own, *near, far])
-            second, _ = after((second, came))
             came = swap(second, 0)
-            sums, *gives = split(keep, got)
+            sums, *gives = split(keep, across(give))
             done = [sums] + deliver(gives)
             second = join(second, came)
-            second, *done = after((second, *done))
-            came = swap(second, 1)
+            second, done[1] = after((second, done[1]))
+            came, *done = after((swap(second, 1), *done))
             keep, give = residual(second, came, parts[1])
-            sums, *gives = split(keep, lax.ppermute(give, AXES, swap_core))
+            sums, *gives = split(keep, across(give))
             done += [sums] + deliver(gives)
             return call(
                 functools.partial(final_kernel, places),
@@ -264,11 +288,12 @@
                 *done,
             )
 
-        own, most = picked(1, 0, pair_offsets, (jax.ShapeDtypeStruct((1,), jnp.int32),))
+        keep, give, most = picked(1, 0, pair_offsets, (jax.ShapeDtypeStruct((1,), jnp.int32),))
+        own = merged(keep, give)
         return lax.cond(
             most[0] <= 2,
             lambda own: rest(1, own),
-            lambda own: rest((blocks + 1) // 2, *picked((blocks + 1) // 2, 0, pair_offsets)),
+            lambda own: rest((blocks + 1) // 2, merged(*picked((blocks + 1) // 2, 0, pair_offsets))),
             own,
         )
 

time: 98 us -> 88.1 us (0.90)
  waiting for transfers between devices: 53.1 us -> 43.7 us
    ppermute x4, waiting for transfers between devices: 19.4 us -> 13.5 us  [swap(): came = lax.ppermute(block.astype(jnp.float16), AXES, in_plane[j])]
    ppermute x6, waiting for transfers between devices: 9.85 us -> 6.89 us  [deliver(): return [lax.ppermute(g, AXES, jumps[j]) for j, g in enumerate(gives, 1)]]
    ppermute x6, waiting for transfers between devices: 17.7 us -> 16.7 us  [jump(): return lax.ppermute(own, AXES, jumps[j])]
    ppermute x12, starting transfers between devices: 2.77 us -> 1.76 us  [the longest x10 1.17 us: across(): return lax.ppermute(m, AXES, swap_core)]
  transfers between devices with their start and end apart: 28 -> 28, of which waited for: 21 -> 19; matrix products, arithmetic and copies ran while one was open for 0% -> 0% of each run, Pallas kernels for 4% -> 4%
where the time goes in v1:
time: 88.1 us; the launch traced here: 88 us
  waiting for transfers between devices  43.7 us (50%)
  starting transfers between devices  30.9 us (35%)
  Pallas kernels  10.7 us (12%)
    ppermute x6, waiting for transfers between devices, jump(): return lax.ppermute(own, AXES, jumps[j])  16.7 us
    ppermute x6, starting transfers between devices, jump(): return lax.ppermute(own, AXES, jumps[j])  13.5 us
    ppermute x4, waiting for transfers between devices, swap(): came = lax.ppermute(block.astype(jnp.float16), AXES, in_plane[j])  13.5 us
    ppermute x6, starting transfers between devices, deliver(): return [lax.ppermute(g, AXES, jumps[j]) for j, g in enumerate(gives, 1)]  10.8 us
    pallas_call x11, Pallas kernels, call(): pl.pallas_call(kernel, out_shape=outs, out_specs=jax.tree.map(place, outs...  10.7 us
    ppermute x6, waiting for transfers between devices, deliver(): return [lax.ppermute(g, AXES, jumps[j]) for j, g in enumerate(gives, 1)]  6.89 us
    ppermute x10, waiting for transfers between devices, across(): return lax.ppermute(m, AXES, swap_core)  4.89 us
    ppermute x4, starting transfers between devices, swap(): came = lax.ppermute(block.astype(jnp.float16), AXES, in_plane[j])  4.89 us
  transfers between devices with their start and end apart: 28, of which 19 were waited for; matrix products, arithmetic and copies ran while one was open for 0% of the time, Pallas kernels for 4%

profile of v1, /device:TPU:0, one launch (start us, length us, event | category | flops | bytes accessed | tf_op | source)
XLA Modules:
  0.0 88.0 jit_solution(18231480785155441795)
XLA Ops:
  0.0 3.0 %shard_map.39 = (bf16[1,80,1500]{2,1,0:T(8,128)(2,1)S(1)}, bf16[1,80,1500]{2,1,0:T(8,128)(2,1)S(1)}, s32[1]{0:T(128)}) custom-call(s32[4]{0:T(128)} %offsets.1, bf16[1500,1024]{1,0:T(8,128)(2,1)} %chol.1), custom_call_target="tpu_custom_call" | custom-call | bytes 3072016 | tf_op jit(solution)/shard_map/pallas_call | solution.py:150
  3.0 0.5 collective-permute-start.55
  4.2 0.5 collective-permute-done.55
  4.7 82.6 %conditional.1 = (f32[64,1024]{1,0:T(8,128)S(1)}) conditional(s32[]{:T(128)} %bitcast, (s32[4]{0:T(128)S(1)}, bf16[1500,1024]{1,0:T(8,128)(2,1)S(1)}, bf16[1024,1024]{1,0:T(8,128)(2,1)}) %tuple.36, (bf16[1,80,1500]{2,1,0:T(8,128)(2,1)S(1)}, bf16[1,80,1500]{2,1,0:T(8,128)(2,1)S(1)}, s32[4]{0:T(128)S(1)}, bf16[1500,1024]{1,0:T(8,128)(2,1)S(1)}, ...), branch_computations={%region_0.0_spmd, %region_1.0_spmd} | conditional | flops 2649218048 | bytes 97610952 | solution.py:293
  4.7 0.1 add.11.refs_0_
  4.7 4.0 %collective-permute-start.28 = (bf16[1,80,1500]{2,1,0:T(8,128)(2,1)S(1)}, bf16[1,80,1500]{2,1,0:T(8,128)(2,1)S(1)}, u32[]{:S(2)}, u32[]{:S(2)}) collective-permute-start(bf16[1,80,1500]{2,1,0:T(8,128)(2,1)S(1)} %add.11.refs_0_), channel_id=1, source_target_pairs={{0,4},{1,5},{2,6},{3,7},{4,0},{5,1},{6,2},{7,3},{8,12},{9,13},{10,... | collective-permute-start | bytes 720008 | tf_op jit(solution)/shard_map/cond/branch_1_fun/ppermute | solution.py:201
  8.8 1.6 %collective-permute-start.29 = (bf16[1,80,1500]{2,1,0:T(8,128)(2,1)S(1)}, bf16[1,80,1500]{2,1,0:T(8,128)(2,1)S(1)}, u32[]{:S(2)}, u32[]{:S(2)}) collective-permute-start(bf16[1,80,1500]{2,1,0:T(8,128)(2,1)S(1)} %add.11.refs_0_), channel_id=1, source_target_pairs={{0,2},{1,3},{2,0},{3,1},{4,6},{5,7},{6,4},{7,5},{8,10},{9,11},{10,... | collective-permute-start | bytes 720008 | tf_op jit(solution)/shard_map/cond/branch_1_fun/ppermute | solution.py:201
  10.3 10.0 %collective-permute-done.28.refs_2_ = bf16[1,80,1500]{2,1,0:T(8,128)(2,1)S(1)} collective-permute-done((bf16[1,80,1500]{2,1,0:T(8,128)(2,1)S(1)}, bf16[1,80,1500]{2,1,0:T(8,128)(2,1)S(1)}, u32[]{:S(2)}, u32[]{:S(2)}) %collective-permute-start.28) | collective-permute-done | bytes 240032 | tf_op jit(solution)/shard_map/cond/branch_1_fun/ppermute | solution.py:201
  20.4 0.2 collective-permute-done.29.refs_1_
  20.6 1.5 %collective-permute-start.31 = (bf16[1,80,1500]{2,1,0:T(8,128)(2,1)S(1)}, bf16[1,80,1500]{2,1,0:T(8,128)(2,1)S(1)}, u32[]{:S(2)}, u32[]{:S(2)}) collective-permute-start(bf16[1,80,1500]{2,1,0:T(8,128)(2,1)S(1)} %collective-permute-done.28.refs_2_), channel_id=1, source_target_pairs={{0,2},{1,3},{2,0},{3,1},{4,6},{5,7},{6,4},{7,5},{8,10},{9,11},{10,... | collective-permute-start | bytes 720008 | tf_op jit(solution)/shard_map/cond/branch_1_fun/ppermute | solution.py:201
  22.1 0.0 collective-permute-start.33
  22.1 0.5 collective-permute-start.34
  22.6 1.5 %branch_1_fun.10 = (bf16[1,48,1500]{2,1,0:T(8,128)(2,1)S(1)}, bf16[1,48,1500]{2,1,0:T(8,128)(2,1)S(1)}) custom-call(s32[4]{0:T(128)S(1)} %get-tuple-element.70.offsets, bf16[1500,1024]{1,0:T(8,128)(2,1)S(1)} %get-tuple-element.71.chol.refs_8_), custom_call_target="tpu_custom_call" | custom-call | bytes 3072016 | tf_op jit(solution)/shard_map/cond/branch_1_fun/pallas_call | solution.py:150
  24.1 0.1 collective-permute-start.30
  24.2 1.4 %collective-permute-done.30 = bf16[1,48,1500]{2,1,0:T(8,128)(2,1)S(1)} collective-permute-done((bf16[1,48,1500]{2,1,0:T(8,128)(2,1)S(1)}, bf16[1,48,1500]{2,1,0:T(8,128)(2,1)S(1)}, u32[]{:S(2)}, u32[]{:S(2)}) %collective-permute-start.30) | collective-permute-done | bytes 144032 | tf_op jit(solution)/shard_map/cond/branch_1_fun/ppermute | solution.py:197
  25.6 2.2 %collective-permute-done.31.refs_3_ = bf16[1,80,1500]{2,1,0:T(8,128)(2,1)S(1)} collective-permute-done((bf16[1,80,1500]{2,1,0:T(8,128)(2,1)S(1)}, bf16[1,80,1500]{2,1,0:T(8,128)(2,1)S(1)}, u32[]{:S(2)}, u32[]{:S(2)}) %collective-permute-start.31) | collective-permute-done | bytes 240032 | tf_op jit(solution)/shard_map/cond/branch_1_fun/ppermute | solution.py:201
  27.8 1.5 %collective-permute-done.35.refs_7_ = bf16[1,80,1500]{2,1,0:T(8,128)(2,1)S(1)} collective-permute-done((bf16[1,80,1500]{2,1,0:T(8,128)(2,1)S(1)}, bf16[1,80,1500]{2,1,0:T(8,128)(2,1)S(1)}, u32[]{:S(2)}, u32[]{:S(2)}) %collective-permute-start.35) | collective-permute-done | bytes 240032 | tf_op jit(solution)/shard_map/cond/branch_1_fun/ppermute | solution.py:204
  29.3 2.4 %branch_1_fun.11.own = f32[336,1024]{1,0:T(8,128)S(1)} custom-call(s32[4]{0:T(128)S(1)} %get-tuple-element.70.offsets, bf16[1,80,1500]{2,1,0:T(8,128)(2,1)S(1)} %add.11.refs_0_, bf16[1,80,1500]{2,1,0:T(8,128)(2,1)S(1)} %collective-permute-done.29.refs_1_, bf16[1,80,1500]{2,1,0:T(8,128)(2,1)S(1)} %collective-permute-done.28.refs_2_, ...), custom_call_target="tpu_custom_call" | custom-call | flops 983040000 | bytes 4992016 | tf_op jit(solution)/shard_map/cond/branch_1_fun/pallas_call | solution.py:150
  31.7 0.1 convert_element_type.44
  31.8 1.3 %collective-permute-start.36 = (f16[336,1024]{1,0:T(8,128)(2,1)S(1)}, f16[336,1024]{1,0:T(8,128)(2,1)S(1)}, u32[]{:S(2)}, u32[]{:S(2)}) collective-permute-start(f16[336,1024]{1,0:T(8,128)(2,1)S(1)} %convert_element_type.44), channel_id=1, source_target_pairs={{0,8},{1,17},{2,10},{3,19},{4,12},{5,21},{6,14},{7,23},{8,0},{9,25... | collective-permute-start | bytes 2064392 | tf_op jit(solution)/shard_map/cond/branch_1_fun/ppermute | solution.py:221
  33.1 3.0 %collective-permute-start.37 = (bf16[1,48,1500]{2,1,0:T(8,128)(2,1)S(1)}, bf16[1,48,1500]{2,1,0:T(8,128)(2,1)S(1)}, u32[]{:S(2)}, u32[]{:S(2)}) collective-permute-start(bf16[1,48,1500]{2,1,0:T(8,128)(2,1)S(1)} %add.12.refs_0_), channel_id=1, source_target_pairs={{0,4},{1,5},{2,6},{3,7},{4,0},{5,1},{6,2},{7,3},{8,12},{9,13},{10,... | collective-permute-start | bytes 432008 | tf_op jit(solution)/shard_map/cond/branch_1_fun/ppermute | solution.py:201
  36.1 1.7 %collective-permute-start.38 = (bf16[1,48,1500]{2,1,0:T(8,128)(2,1)S(1)}, bf16[1,48,1500]{2,1,0:T(8,128)(2,1)S(1)}, u32[]{:S(2)}, u32[]{:S(2)}) collective-permute-start(bf16[1,48,1500]{2,1,0:T(8,128)(2,1)S(1)} %add.12.refs_0_), channel_id=1, source_target_pairs={{0,2},{1,3},{2,0},{3,1},{4,6},{5,7},{6,4},{7,5},{8,10},{9,11},{10,... | collective-permute-start | bytes 432008 | tf_op jit(solution)/shard_map/cond/branch_1_fun/ppermute | solution.py:201
  37.9 5.0 %collective-permute-done.36 = f16[336,1024]{1,0:T(8,128)(2,1)S(1)} collective-permute-done((f16[336,1024]{1,0:T(8,128)(2,1)S(1)}, f16[336,1024]{1,0:T(8,128)(2,1)S(1)}, u32[]{:S(2)}, u32[]{:S(2)}) %collective-permute-start.36) | collective-permute-done | bytes 688160 | tf_op jit(solution)/shard_map/cond/branch_1_fun/ppermute | solution.py:221
  42.8 0.1 convert_element_type.45.came
  43.0 0.3 collective-permute-done.37.refs_2_
  43.3 0.1 collective-permute-done.38.refs_1_
  43.3 0.2 branch_1_fun.12.own
  43.5 0.1 convert_element_type.46
  43.6 0.9 %collective-permute-start.44 = (f16[336,1024]{1,0:T(8,128)(2,1)S(1)}, f16[336,1024]{1,0:T(8,128)(2,1)S(1)}, u32[]{:S(2)}, u32[]{:S(2)}) collective-permute-start(f16[336,1024]{1,0:T(8,128)(2,1)S(1)} %convert_element_type.46), channel_id=1, source_target_pairs={{0,16},{1,9},{2,18},{3,11},{4,20},{5,13},{6,22},{7,15},{8,24},{9,1... | collective-permute-start | bytes 2064392 | tf_op jit(solution)/shard_map/cond/branch_1_fun/ppermute | solution.py:221
  44.6 1.7 %collective-permute-start.39 = (bf16[1,48,1500]{2,1,0:T(8,128)(2,1)S(1)}, bf16[1,48,1500]{2,1,0:T(8,128)(2,1)S(1)}, u32[]{:S(2)}, u32[]{:S(2)}) collective-permute-start(bf16[1,48,1500]{2,1,0:T(8,128)(2,1)S(1)} %collective-permute-done.37.refs_2_), channel_id=1, source_target_pairs={{0,2},{1,3},{2,0},{3,1},{4,6},{5,7},{6,4},{7,5},{8,10},{9,11},{10,... | collective-permute-start | bytes 432008 | tf_op jit(solution)/shard_map/cond/branch_1_fun/ppermute | solution.py:201
  46.3 0.5 collective-permute-start.42
  46.8 3.8 %collective-permute-done.39.refs_3_ = bf16[1,48,1500]{2,1,0:T(8,128)(2,1)S(1)} collective-permute-done((bf16[1,48,1500]{2,1,0:T(8,128)(2,1)S(1)}, bf16[1,48,1500]{2,1,0:T(8,128)(2,1)S(1)}, u32[]{:S(2)}, u32[]{:S(2)}) %collective-permute-start.39) | collective-permute-done | bytes 144032 | tf_op jit(solution)/shard_map/cond/branch_1_fun/ppermute | solution.py:201
  50.6 1.3 %collective-permute-done.43.refs_7_ = bf16[1,48,1500]{2,1,0:T(8,128)(2,1)S(1)} collective-permute-done((bf16[1,48,1500]{2,1,0:T(8,128)(2,1)S(1)}, bf16[1,48,1500]{2,1,0:T(8,128)(2,1)S(1)}, u32[]{:S(2)}, u32[]{:S(2)}) %collective-permute-start.43) | collective-permute-done | bytes 144032 | tf_op jit(solution)/shard_map/cond/branch_1_fun/ppermute | solution.py:204
  52.0 1.7 %branch_1_fun.13.own = f32[208,1024]{1,0:T(8,128)S(1)} custom-call(s32[4]{0:T(128)S(1)} %get-tuple-element.70.offsets, bf16[1,48,1500]{2,1,0:T(8,128)(2,1)S(1)} %add.12.refs_0_, bf16[1,48,1500]{2,1,0:T(8,128)(2,1)S(1)} %collective-permute-done.38.refs_1_, bf16[1,48,1500]{2,1,0:T(8,128)(2,1)S(1)} %collective-permute-done.37.refs_2_, ...), custom_call_target="tpu_custom_call" | custom-call | flops 589824000 | bytes 4224016 | tf_op jit(solution)/shard_map/cond/branch_1_fun/pallas_call | solution.py:150
  53.7 1.0 %collective-permute-done.44 = f16[336,1024]{1,0:T(8,128)(2,1)S(1)} collective-permute-done((f16[336,1024]{1,0:T(8,128)(2,1)S(1)}, f16[336,1024]{1,0:T(8,128)(2,1)S(1)}, u32[]{:S(2)}, u32[]{:S(2)}) %collective-permute-start.44) | collective-permute-done | bytes 688160 | tf_op jit(solution)/shard_map/cond/branch_1_fun/ppermute | solution.py:221
  54.6 0.1 convert_element_type.47.came
  54.7 1.0 %branch_1_fun.15 = (f32[4,40,1024]{2,1,0:T(8,128)S(1)}, f32[4,40,1024]{2,1,0:T(8,128)S(1)}) custom-call(f32[336,1024]{1,0:T(8,128)S(1)} %branch_1_fun.12.own, f32[336,1024]{1,0:T(8,128)S(1)} %convert_element_type.47.came, bf16[1024,1024]{1,0:T(8,128)(2,1)S(1)} %copy-done.2), custom_call_target="tpu_custom_call" | custom-call | flops 671088640 | bytes 4849664 | tf_op jit(solution)/shard_map/cond/branch_1_fun/pallas_call | solution.py:150
  55.8 0.1 collective-permute-start.46
  55.8 0.1 convert_element_type.48
  55.9 1.7 %collective-permute-start.45 = (f16[208,1024]{1,0:T(8,128)(2,1)S(1)}, f16[208,1024]{1,0:T(8,128)(2,1)S(1)}, u32[]{:S(2)}, u32[]{:S(2)}) collective-permute-start(f16[208,1024]{1,0:T(8,128)(2,1)S(1)} %convert_element_type.48), channel_id=1, source_target_pairs={{0,8},{1,17},{2,10},{3,19},{4,12},{5,21},{6,14},{7,23},{8,0},{9,25... | collective-permute-start | bytes 1277960 | tf_op jit(solution)/shard_map/cond/branch_1_fun/ppermute | solution.py:221
  57.6 0.3 collective-permute-done.46.came
  57.9 0.1 branch_1_fun.16
  58.0 1.7 %collective-permute-start.47 = (bf16[40,1024]{1,0:T(8,128)(2,1)S(1)}, bf16[40,1024]{1,0:T(8,128)(2,1)S(1)}, u32[]{:S(2)}, u32[]{:S(2)}) collective-permute-start(bf16[40,1024]{1,0:T(8,128)(2,1)S(1)} %get-tuple-element.88), channel_id=1, source_target_pairs={{0,2},{1,3},{2,0},{3,1},{4,6},{5,7},{6,4},{7,5},{8,10},{9,11},{10,... | collective-permute-start | bytes 245768 | tf_op jit(solution)/shard_map/cond/branch_1_fun/ppermute | solution.py:252
  59.7 4.4 %collective-permute-done.45 = f16[208,1024]{1,0:T(8,128)(2,1)S(1)} collective-permute-done((f16[208,1024]{1,0:T(8,128)(2,1)S(1)}, f16[208,1024]{1,0:T(8,128)(2,1)S(1)}, u32[]{:S(2)}, u32[]{:S(2)}) %collective-permute-start.45) | collective-permute-done | bytes 426016 | tf_op jit(solution)/shard_map/cond/branch_1_fun/ppermute | solution.py:221
  64.1 0.1 convert_element_type.49.came
  64.2 0.1 branch_1_fun.14.own
  64.3 0.1 convert_element_type.50
  64.4 0.9 %collective-permute-start.48 = (f16[208,1024]{1,0:T(8,128)(2,1)S(1)}, f16[208,1024]{1,0:T(8,128)(2,1)S(1)}, u32[]{:S(2)}, u32[]{:S(2)}) collective-permute-start(f16[208,1024]{1,0:T(8,128)(2,1)S(1)} %convert_element_type.50), channel_id=1, source_target_pairs={{0,16},{1,9},{2,18},{3,11},{4,20},{5,13},{6,22},{7,15},{8,24},{9,1... | collective-permute-start | bytes 1277960 | tf_op jit(solution)/shard_map/cond/branch_1_fun/ppermute | solution.py:221
  65.3 3.0 %collective-permute-start.49 = (bf16[40,1024]{1,0:T(8,128)(2,1)S(1)}, bf16[40,1024]{1,0:T(8,128)(2,1)S(1)}, u32[]{:S(2)}, u32[]{:S(2)}) collective-permute-start(bf16[40,1024]{1,0:T(8,128)(2,1)S(1)} %get-tuple-element.92), channel_id=1, source_target_pairs={{0,4},{1,5},{2,6},{3,7},{4,0},{5,1},{6,2},{7,3},{8,12},{9,13},{10,... | collective-permute-start | bytes 245768 | tf_op jit(solution)/shard_map/cond/branch_1_fun/ppermute | solution.py:252
  68.3 1.2 %collective-permute-start.50 = (bf16[40,1024]{1,0:T(8,128)(2,1)S(1)}, bf16[40,1024]{1,0:T(8,128)(2,1)S(1)}, u32[]{:S(2)}, u32[]{:S(2)}) collective-permute-start(bf16[40,1024]{1,0:T(8,128)(2,1)S(1)} %get-tuple-element.93), channel_id=1, source_target_pairs={{0,6},{1,7},{2,4},{3,5},{4,2},{5,3},{6,0},{7,1},{8,14},{9,15},{10,... | collective-permute-start | bytes 245768 | tf_op jit(solution)/shard_map/cond/branch_1_fun/ppermute | solution.py:252
  69.5 3.1 %collective-permute-done.48 = f16[208,1024]{1,0:T(8,128)(2,1)S(1)} collective-permute-done((f16[208,1024]{1,0:T(8,128)(2,1)S(1)}, f16[208,1024]{1,0:T(8,128)(2,1)S(1)}, u32[]{:S(2)}, u32[]{:S(2)}) %collective-permute-start.48) | collective-permute-done | bytes 426016 | tf_op jit(solution)/shard_map/cond/branch_1_fun/ppermute | solution.py:221
  72.5 0.1 convert_element_type.51.came
  72.6 2.1 %collective-permute-done.49.refs_2_ = bf16[40,1024]{1,0:T(8,128)(2,1)S(1)} collective-permute-done((bf16[40,1024]{1,0:T(8,128)(2,1)S(1)}, bf16[40,1024]{1,0:T(8,128)(2,1)S(1)}, u32[]{:S(2)}, u32[]{:S(2)}) %collective-permute-start.49) | collective-permute-done | bytes 81952 | tf_op jit(solution)/shard_map/cond/branch_1_fun/ppermute | solution.py:252
  74.7 0.7 branch_1_fun.17
  75.5 0.1 collective-permute-start.51
  75.5 1.7 %collective-permute-done.51.came = f32[4,24,1024]{2,1,0:T(8,128)S(1)} collective-permute-done((f32[4,24,1024]{2,1,0:T(8,128)S(1)}, f32[4,24,1024]{2,1,0:T(8,128)S(1)}, u32[]{:S(2)}, u32[]{:S(2)}) %collective-permute-start.51) | collective-permute-done | bytes 393248 | tf_op jit(solution)/shard_map/cond/branch_1_fun/ppermute | solution.py:204
  77.3 1.8 %collective-permute-start.52 = (bf16[24,1024]{1,0:T(8,128)(2,1)S(1)}, bf16[24,1024]{1,0:T(8,128)(2,1)S(1)}, u32[]{:S(2)}, u32[]{:S(2)}) collective-permute-start(bf16[24,1024]{1,0:T(8,128)(2,1)S(1)} %get-tuple-element.102), channel_id=1, source_target_pairs={{0,2},{1,3},{2,0},{3,1},{4,6},{5,7},{6,4},{7,5},{8,10},{9,11},{10,... | collective-permute-start | bytes 147464 | tf_op jit(solution)/shard_map/cond/branch_1_fun/ppermute | solution.py:252
  79.1 1.9 %collective-permute-start.53 = (bf16[24,1024]{1,0:T(8,128)(2,1)S(1)}, bf16[24,1024]{1,0:T(8,128)(2,1)S(1)}, u32[]{:S(2)}, u32[]{:S(2)}) collective-permute-start(bf16[24,1024]{1,0:T(8,128)(2,1)S(1)} %get-tuple-element.103), channel_id=1, source_target_pairs={{0,4},{1,5},{2,6},{3,7},{4,0},{5,1},{6,2},{7,3},{8,12},{9,13},{10,... | collective-permute-start | bytes 147464 | tf_op jit(solution)/shard_map/cond/branch_1_fun/ppermute | solution.py:252
  81.0 1.2 %collective-permute-start.54 = (bf16[24,1024]{1,0:T(8,128)(2,1)S(1)}, bf16[24,1024]{1,0:T(8,128)(2,1)S(1)}, u32[]{:S(2)}, u32[]{:S(2)}) collective-permute-start(bf16[24,1024]{1,0:T(8,128)(2,1)S(1)} %get-tuple-element.104), channel_id=1, source_target_pairs={{0,6},{1,7},{2,4},{3,5},{4,2},{5,3},{6,0},{7,1},{8,14},{9,15},{10,... | collective-permute-start | bytes 147464 | tf_op jit(solution)/shard_map/cond/branch_1_fun/ppermute | solution.py:252
  82.2 3.5 %collective-permute-done.53.refs_6_ = bf16[24,1024]{1,0:T(8,128)(2,1)S(1)} collective-permute-done((bf16[24,1024]{1,0:T(8,128)(2,1)S(1)}, bf16[24,1024]{1,0:T(8,128)(2,1)S(1)}, u32[]{:S(2)}, u32[]{:S(2)}) %collective-permute-start.53) | collective-permute-done | bytes 49184 | tf_op jit(solution)/shard_map/cond/branch_1_fun/ppermute | solution.py:252
  85.7 1.3 %collective-permute-done.54.refs_7_ = bf16[24,1024]{1,0:T(8,128)(2,1)S(1)} collective-permute-done((bf16[24,1024]{1,0:T(8,128)(2,1)S(1)}, bf16[24,1024]{1,0:T(8,128)(2,1)S(1)}, u32[]{:S(2)}, u32[]{:S(2)}) %collective-permute-start.54) | collective-permute-done | bytes 49184 | tf_op jit(solution)/shard_map/cond/branch_1_fun/ppermute | solution.py:252
  87.0 0.1 branch_1_fun.19
  87.3 0.0 copy-start.3
  87.3 0.7 copy-done.3
  (22 shorter events, 0.1 us)
Async XLA Ops:
  0.0 4.7 %copy-start.4 = (s32[4]{0:T(128)S(1)}, s32[4]{0:T(128)}, u32[]{:S(2)}) copy-start(s32[4]{0:T(128)} %offsets.1) | copy-start | bytes 52
  0.0 4.7 %copy-start = (bf16[1500,1024]{1,0:T(8,128)(2,1)S(1)}, bf16[1500,1024]{1,0:T(8,128)(2,1)}, u32[]{:S(2)}) copy-start(bf16[1500,1024]{1,0:T(8,128)(2,1)} %chol.1) | copy-start | bytes 9216004
  3.0 1.7 %collective-permute-start.55 = (bf16[1,80,1500]{2,1,0:T(8,128)(2,1)S(1)}, bf16[1,80,1500]{2,1,0:T(8,128)(2,1)S(1)}, u32[]{:S(2)}, u32[]{:S(2)}) collective-permute-start(bf16[1,80,1500]{2,1,0:T(8,128)(2,1)S(1)} %get-tuple-element.110), channel_id=1, source_target_pairs={{0,1},{1,0},{2,3},{3,2},{4,5},{5,4},{6,7},{7,6},{8,9},{9,8},{10,11... | collective-permute-start | bytes 720008 | tf_op jit(solution)/shard_map/ppermute | solution.py:197
  4.7 15.7 %collective-permute-start.28 = (bf16[1,80,1500]{2,1,0:T(8,128)(2,1)S(1)}, bf16[1,80,1500]{2,1,0:T(8,128)(2,1)S(1)}, u32[]{:S(2)}, u32[]{:S(2)}) collective-permute-start(bf16[1,80,1500]{2,1,0:T(8,128)(2,1)S(1)} %add.11.refs_0_), channel_id=1, source_target_pairs={{0,4},{1,5},{2,6},{3,7},{4,0},{5,1},{6,2},{7,3},{8,12},{9,13},{10,... | collective-permute-start | bytes 720008 | tf_op jit(solution)/shard_map/cond/branch_1_fun/ppermute | solution.py:201
  8.8 11.8 %collective-permute-start.29 = (bf16[1,80,1500]{2,1,0:T(8,128)(2,1)S(1)}, bf16[1,80,1500]{2,1,0:T(8,128)(2,1)S(1)}, u32[]{:S(2)}, u32[]{:S(2)}) collective-permute-start(bf16[1,80,1500]{2,1,0:T(8,128)(2,1)S(1)} %add.11.refs_0_), channel_id=1, source_target_pairs={{0,2},{1,3},{2,0},{3,1},{4,6},{5,7},{6,4},{7,5},{8,10},{9,11},{10,... | collective-permute-start | bytes 720008 | tf_op jit(solution)/shard_map/cond/branch_1_fun/ppermute | solution.py:201
  10.3 15.3 %collective-permute-start.32 = (bf16[1,80,1500]{2,1,0:T(8,128)(2,1)S(1)}, bf16[1,80,1500]{2,1,0:T(8,128)(2,1)S(1)}, u32[]{:S(2)}, u32[]{:S(2)}) collective-permute-start(bf16[1,80,1500]{2,1,0:T(8,128)(2,1)S(1)} %add.11.refs_0_), channel_id=1, source_target_pairs={{0,1},{1,0},{2,3},{3,2},{4,5},{5,4},{6,7},{7,6},{8,9},{9,8},{10,11... | collective-permute-start | bytes 720008 | tf_op jit(solution)/shard_map/cond/branch_1_fun/ppermute | solution.py:204
  20.6 7.2 %collective-permute-start.31 = (bf16[1,80,1500]{2,1,0:T(8,128)(2,1)S(1)}, bf16[1,80,1500]{2,1,0:T(8,128)(2,1)S(1)}, u32[]{:S(2)}, u32[]{:S(2)}) collective-permute-start(bf16[1,80,1500]{2,1,0:T(8,128)(2,1)S(1)} %collective-permute-done.28.refs_2_), channel_id=1, source_target_pairs={{0,2},{1,3},{2,0},{3,1},{4,6},{5,7},{6,4},{7,5},{8,10},{9,11},{10,... | collective-permute-start | bytes 720008 | tf_op jit(solution)/shard_map/cond/branch_1_fun/ppermute | solution.py:201
  22.1 5.8 %collective-permute-start.33 = (bf16[1,80,1500]{2,1,0:T(8,128)(2,1)S(1)}, bf16[1,80,1500]{2,1,0:T(8,128)(2,1)S(1)}, u32[]{:S(2)}, u32[]{:S(2)}) collective-permute-start(bf16[1,80,1500]{2,1,0:T(8,128)(2,1)S(1)} %collective-permute-done.29.refs_1_), channel_id=1, source_target_pairs={{0,1},{1,0},{2,3},{3,2},{4,5},{5,4},{6,7},{7,6},{8,9},{9,8},{10,11... | collective-permute-start | bytes 720008 | tf_op jit(solution)/shard_map/cond/branch_1_fun/ppermute | solution.py:204
  22.1 5.8 %collective-permute-start.34 = (bf16[1,80,1500]{2,1,0:T(8,128)(2,1)S(1)}, bf16[1,80,1500]{2,1,0:T(8,128)(2,1)S(1)}, u32[]{:S(2)}, u32[]{:S(2)}) collective-permute-start(bf16[1,80,1500]{2,1,0:T(8,128)(2,1)S(1)} %collective-permute-done.28.refs_2_), channel_id=1, source_target_pairs={{0,1},{1,0},{2,3},{3,2},{4,5},{5,4},{6,7},{7,6},{8,9},{9,8},{10,11... | collective-permute-start | bytes 720008 | tf_op jit(solution)/shard_map/cond/branch_1_fun/ppermute | solution.py:204
  24.1 1.4 %collective-permute-start.30 = (bf16[1,48,1500]{2,1,0:T(8,128)(2,1)S(1)}, bf16[1,48,1500]{2,1,0:T(8,128)(2,1)S(1)}, u32[]{:S(2)}, u32[]{:S(2)}) collective-permute-start(bf16[1,48,1500]{2,1,0:T(8,128)(2,1)S(1)} %get-tuple-element.73), channel_id=1, source_target_pairs={{0,1},{1,0},{2,3},{3,2},{4,5},{5,4},{6,7},{7,6},{8,9},{9,8},{10,11... | collective-permute-start | bytes 432008 | tf_op jit(solution)/shard_map/cond/branch_1_fun/ppermute | solution.py:197
  27.8 1.5 %collective-permute-start.35 = (bf16[1,80,1500]{2,1,0:T(8,128)(2,1)S(1)}, bf16[1,80,1500]{2,1,0:T(8,128)(2,1)S(1)}, u32[]{:S(2)}, u32[]{:S(2)}) collective-permute-start(bf16[1,80,1500]{2,1,0:T(8,128)(2,1)S(1)} %collective-permute-done.31.refs_3_), channel_id=1, source_target_pairs={{0,1},{1,0},{2,3},{3,2},{4,5},{5,4},{6,7},{7,6},{8,9},{9,8},{10,11... | collective-permute-start | bytes 720008 | tf_op jit(solution)/shard_map/cond/branch_1_fun/ppermute | solution.py:204
  31.8 11.0 %collective-permute-start.36 = (f16[336,1024]{1,0:T(8,128)(2,1)S(1)}, f16[336,1024]{1,0:T(8,128)(2,1)S(1)}, u32[]{:S(2)}, u32[]{:S(2)}) collective-permute-start(f16[336,1024]{1,0:T(8,128)(2,1)S(1)} %convert_element_type.44), channel_id=1, source_target_pairs={{0,8},{1,17},{2,10},{3,19},{4,12},{5,21},{6,14},{7,23},{8,0},{9,25... | collective-permute-start | bytes 2064392 | tf_op jit(solution)/shard_map/cond/branch_1_fun/ppermute | solution.py:221
  33.1 10.2 %collective-permute-start.37 = (bf16[1,48,1500]{2,1,0:T(8,128)(2,1)S(1)}, bf16[1,48,1500]{2,1,0:T(8,128)(2,1)S(1)}, u32[]{:S(2)}, u32[]{:S(2)}) collective-permute-start(bf16[1,48,1500]{2,1,0:T(8,128)(2,1)S(1)} %add.12.refs_0_), channel_id=1, source_target_pairs={{0,4},{1,5},{2,6},{3,7},{4,0},{5,1},{6,2},{7,3},{8,12},{9,13},{10,... | collective-permute-start | bytes 432008 | tf_op jit(solution)/shard_map/cond/branch_1_fun/ppermute | solution.py:201
  36.1 7.2 %collective-permute-start.38 = (bf16[1,48,1500]{2,1,0:T(8,128)(2,1)S(1)}, bf16[1,48,1500]{2,1,0:T(8,128)(2,1)S(1)}, u32[]{:S(2)}, u32[]{:S(2)}) collective-permute-start(bf16[1,48,1500]{2,1,0:T(8,128)(2,1)S(1)} %add.12.refs_0_), channel_id=1, source_target_pairs={{0,2},{1,3},{2,0},{3,1},{4,6},{5,7},{6,4},{7,5},{8,10},{9,11},{10,... | collective-permute-start | bytes 432008 | tf_op jit(solution)/shard_map/cond/branch_1_fun/ppermute | solution.py:201
  43.6 11.0 %collective-permute-start.44 = (f16[336,1024]{1,0:T(8,128)(2,1)S(1)}, f16[336,1024]{1,0:T(8,128)(2,1)S(1)}, u32[]{:S(2)}, u32[]{:S(2)}) collective-permute-start(f16[336,1024]{1,0:T(8,128)(2,1)S(1)} %convert_element_type.46), channel_id=1, source_target_pairs={{0,16},{1,9},{2,18},{3,11},{4,20},{5,13},{6,22},{7,15},{8,24},{9,1... | collective-permute-start | bytes 2064392 | tf_op jit(solution)/shard_map/cond/branch_1_fun/ppermute | solution.py:221
  44.6 6.0 %collective-permute-start.39 = (bf16[1,48,1500]{2,1,0:T(8,128)(2,1)S(1)}, bf16[1,48,1500]{2,1,0:T(8,128)(2,1)S(1)}, u32[]{:S(2)}, u32[]{:S(2)}) collective-permute-start(bf16[1,48,1500]{2,1,0:T(8,128)(2,1)S(1)} %collective-permute-done.37.refs_2_), channel_id=1, source_target_pairs={{0,2},{1,3},{2,0},{3,1},{4,6},{5,7},{6,4},{7,5},{8,10},{9,11},{10,... | collective-permute-start | bytes 432008 | tf_op jit(solution)/shard_map/cond/branch_1_fun/ppermute | solution.py:201
  46.2 4.3 %collective-permute-start.40 = (bf16[1,48,1500]{2,1,0:T(8,128)(2,1)S(1)}, bf16[1,48,1500]{2,1,0:T(8,128)(2,1)S(1)}, u32[]{:S(2)}, u32[]{:S(2)}) collective-permute-start(bf16[1,48,1500]{2,1,0:T(8,128)(2,1)S(1)} %add.12.refs_0_), channel_id=1, source_target_pairs={{0,1},{1,0},{2,3},{3,2},{4,5},{5,4},{6,7},{7,6},{8,9},{9,8},{10,11... | collective-permute-start | bytes 432008 | tf_op jit(solution)/shard_map/cond/branch_1_fun/ppermute | solution.py:204
  46.3 4.3 %collective-permute-start.42 = (bf16[1,48,1500]{2,1,0:T(8,128)(2,1)S(1)}, bf16[1,48,1500]{2,1,0:T(8,128)(2,1)S(1)}, u32[]{:S(2)}, u32[]{:S(2)}) collective-permute-start(bf16[1,48,1500]{2,1,0:T(8,128)(2,1)S(1)} %collective-permute-done.37.refs_2_), channel_id=1, source_target_pairs={{0,1},{1,0},{2,3},{3,2},{4,5},{5,4},{6,7},{7,6},{8,9},{9,8},{10,11... | collective-permute-start | bytes 432008 | tf_op jit(solution)/shard_map/cond/branch_1_fun/ppermute | solution.py:204
  46.8 3.8 %collective-permute-start.41 = (bf16[1,48,1500]{2,1,0:T(8,128)(2,1)S(1)}, bf16[1,48,1500]{2,1,0:T(8,128)(2,1)S(1)}, u32[]{:S(2)}, u32[]{:S(2)}) collective-permute-start(bf16[1,48,1500]{2,1,0:T(8,128)(2,1)S(1)} %collective-permute-done.38.refs_1_), channel_id=1, source_target_pairs={{0,1},{1,0},{2,3},{3,2},{4,5},{5,4},{6,7},{7,6},{8,9},{9,8},{10,11... | collective-permute-start | bytes 432008 | tf_op jit(solution)/shard_map/cond/branch_1_fun/ppermute | solution.py:204
  50.6 1.4 %collective-permute-start.43 = (bf16[1,48,1500]{2,1,0:T(8,128)(2,1)S(1)}, bf16[1,48,1500]{2,1,0:T(8,128)(2,1)S(1)}, u32[]{:S(2)}, u32[]{:S(2)}) collective-permute-start(bf16[1,48,1500]{2,1,0:T(8,128)(2,1)S(1)} %collective-permute-done.39.refs_3_), channel_id=1, source_target_pairs={{0,1},{1,0},{2,3},{3,2},{4,5},{5,4},{6,7},{7,6},{8,9},{9,8},{10,11... | collective-permute-start | bytes 432008 | tf_op jit(solution)/shard_map/cond/branch_1_fun/ppermute | solution.py:204
  52.0 2.8 %copy-start.2 = (bf16[1024,1024]{1,0:T(8,128)(2,1)S(1)}, bf16[1024,1024]{1,0:T(8,128)(2,1)}, u32[]{:S(2)}) copy-start(bf16[1024,1024]{1,0:T(8,128)(2,1)} %get-tuple-element.85.amplitudes) | copy-start | bytes 6291460 | tf_op jit(solution)/shard_map/cond
  55.8 2.2 %collective-permute-start.46 = (f32[4,40,1024]{2,1,0:T(8,128)S(1)}, f32[4,40,1024]{2,1,0:T(8,128)S(1)}, u32[]{:S(2)}, u32[]{:S(2)}) collective-permute-start(f32[4,40,1024]{2,1,0:T(8,128)S(1)} %get-tuple-element.87), channel_id=1, source_target_pairs={{0,1},{1,0},{2,3},{3,2},{4,5},{5,4},{6,7},{7,6},{8,9},{9,8},{10,11... | collective-permute-start | bytes 1966088 | tf_op jit(solution)/shard_map/cond/branch_1_fun/ppermute | solution.py:204
  55.9 8.2 %collective-permute-start.45 = (f16[208,1024]{1,0:T(8,128)(2,1)S(1)}, f16[208,1024]{1,0:T(8,128)(2,1)S(1)}, u32[]{:S(2)}, u32[]{:S(2)}) collective-permute-start(f16[208,1024]{1,0:T(8,128)(2,1)S(1)} %convert_element_type.48), channel_id=1, source_target_pairs={{0,8},{1,17},{2,10},{3,19},{4,12},{5,21},{6,14},{7,23},{8,0},{9,25... | collective-permute-start | bytes 1277960 | tf_op jit(solution)/shard_map/cond/branch_1_fun/ppermute | solution.py:221
  58.0 6.3 %collective-permute-start.47 = (bf16[40,1024]{1,0:T(8,128)(2,1)S(1)}, bf16[40,1024]{1,0:T(8,128)(2,1)S(1)}, u32[]{:S(2)}, u32[]{:S(2)}) collective-permute-start(bf16[40,1024]{1,0:T(8,128)(2,1)S(1)} %get-tuple-element.88), channel_id=1, source_target_pairs={{0,2},{1,3},{2,0},{3,1},{4,6},{5,7},{6,4},{7,5},{8,10},{9,11},{10,... | collective-permute-start | bytes 245768 | tf_op jit(solution)/shard_map/cond/branch_1_fun/ppermute | solution.py:252
  64.4 8.2 %collective-permute-start.48 = (f16[208,1024]{1,0:T(8,128)(2,1)S(1)}, f16[208,1024]{1,0:T(8,128)(2,1)S(1)}, u32[]{:S(2)}, u32[]{:S(2)}) collective-permute-start(f16[208,1024]{1,0:T(8,128)(2,1)S(1)} %convert_element_type.50), channel_id=1, source_target_pairs={{0,16},{1,9},{2,18},{3,11},{4,20},{5,13},{6,22},{7,15},{8,24},{9,1... | collective-permute-start | bytes 1277960 | tf_op jit(solution)/shard_map/cond/branch_1_fun/ppermute | solution.py:221
  65.3 9.4 %collective-permute-start.49 = (bf16[40,1024]{1,0:T(8,128)(2,1)S(1)}, bf16[40,1024]{1,0:T(8,128)(2,1)S(1)}, u32[]{:S(2)}, u32[]{:S(2)}) collective-permute-start(bf16[40,1024]{1,0:T(8,128)(2,1)S(1)} %get-tuple-element.92), channel_id=1, source_target_pairs={{0,4},{1,5},{2,6},{3,7},{4,0},{5,1},{6,2},{7,3},{8,12},{9,13},{10,... | collective-permute-start | bytes 245768 | tf_op jit(solution)/shard_map/cond/branch_1_fun/ppermute | solution.py:252
  68.3 6.5 %collective-permute-start.50 = (bf16[40,1024]{1,0:T(8,128)(2,1)S(1)}, bf16[40,1024]{1,0:T(8,128)(2,1)S(1)}, u32[]{:S(2)}, u32[]{:S(2)}) collective-permute-start(bf16[40,1024]{1,0:T(8,128)(2,1)S(1)} %get-tuple-element.93), channel_id=1, source_target_pairs={{0,6},{1,7},{2,4},{3,5},{4,2},{5,3},{6,0},{7,1},{8,14},{9,15},{10,... | collective-permute-start | bytes 245768 | tf_op jit(solution)/shard_map/cond/branch_1_fun/ppermute | solution.py:252
  75.5 1.8 %collective-permute-start.51 = (f32[4,24,1024]{2,1,0:T(8,128)S(1)}, f32[4,24,1024]{2,1,0:T(8,128)S(1)}, u32[]{:S(2)}, u32[]{:S(2)}) collective-permute-start(f32[4,24,1024]{2,1,0:T(8,128)S(1)} %get-tuple-element.100), channel_id=1, source_target_pairs={{0,1},{1,0},{2,3},{3,2},{4,5},{5,4},{6,7},{7,6},{8,9},{9,8},{10,11... | collective-permute-start | bytes 1179656 | tf_op jit(solution)/shard_map/cond/branch_1_fun/ppermute | solution.py:204
  77.3 4.9 %collective-permute-start.52 = (bf16[24,1024]{1,0:T(8,128)(2,1)S(1)}, bf16[24,1024]{1,0:T(8,128)(2,1)S(1)}, u32[]{:S(2)}, u32[]{:S(2)}) collective-permute-start(bf16[24,1024]{1,0:T(8,128)(2,1)S(1)} %get-tuple-element.102), channel_id=1, source_target_pairs={{0,2},{1,3},{2,0},{3,1},{4,6},{5,7},{6,4},{7,5},{8,10},{9,11},{10,... | collective-permute-start | bytes 147464 | tf_op jit(solution)/shard_map/cond/branch_1_fun/ppermute | solution.py:252
  79.1 6.6 %collective-permute-start.53 = (bf16[24,1024]{1,0:T(8,128)(2,1)S(1)}, bf16[24,1024]{1,0:T(8,128)(2,1)S(1)}, u32[]{:S(2)}, u32[]{:S(2)}) collective-permute-start(bf16[24,1024]{1,0:T(8,128)(2,1)S(1)} %get-tuple-element.103), channel_id=1, source_target_pairs={{0,4},{1,5},{2,6},{3,7},{4,0},{5,1},{6,2},{7,3},{8,12},{9,13},{10,... | collective-permute-start | bytes 147464 | tf_op jit(solution)/shard_map/cond/branch_1_fun/ppermute | solution.py:252
  81.0 6.0 %collective-permute-start.54 = (bf16[24,1024]{1,0:T(8,128)(2,1)S(1)}, bf16[24,1024]{1,0:T(8,128)(2,1)S(1)}, u32[]{:S(2)}, u32[]{:S(2)}) collective-permute-start(bf16[24,1024]{1,0:T(8,128)(2,1)S(1)} %get-tuple-element.104), channel_id=1, source_target_pairs={{0,6},{1,7},{2,4},{3,5},{4,2},{5,3},{6,0},{7,1},{8,14},{9,15},{10,... | collective-permute-start | bytes 147464 | tf_op jit(solution)/shard_map/cond/branch_1_fun/ppermute | solution.py:252
  87.3 0.7 copy-start.3
